TPU v7x, 128 devices: a whole 4x4x4 slice. The times are simulated.
128 devices in a mesh: grid: 64 (over z, y, x), cell: 2 (over core).
Axes of the slice: x: 4, y: 4, z: 4, core: 2. Of those that a mesh axis runs over, the one named last changes fastest.
Arguments:
- spectrum: bfloat16 [1296, 512, 128], P(None, ('grid', 'cell')), may hold values from 0.049804688 to 1
- depth_factor: float32 [512, 128], P(('grid', 'cell')), may hold values from 0.5 to 1
- wet_mask: int32 [512, 128], P(('grid', 'cell')), may hold values 0 or 1
- frac_index: int32 [512, 128], P(('grid', 'cell')), may hold values from 0 to 3
- boundary_map: int32 [512, 2], P(('grid', 'cell')), may hold values from 0 to 511
- average_map: int32 [512, 128], P(('grid', 'cell')), may hold values from 0 to 511
- dia_plus: int32 [1296], replicated, may hold values from 0 to 1295
- dia_minus: int32 [1296], replicated, may hold values from 0 to 1295
- dia_coef: float32 [36], replicated, may hold values from 0.05 to 10
Outputs:
- spectrum_next: bfloat16 [1296, 512, 128], P(None, ('grid', 'cell'))
Inputs may be any that keep to these rules, and one draw needn't show every extreme that they name: `boundary_map`: indices of parent cells within the strip of the same index. `average_map`: indices of parent cells within the strip of the same index; the parent grid's own entries are not read.
All inputs are finite; a program needn't handle non-finite values. No bound on the sum of `wet_mask` on one device may be relied on, other than what follows from the above.
Results may differ from a plain program's by a relative error of at most 0.0004.
Values may be sent and summed in bfloat16 or wider, within the bound.
No kernel may reach another device: no remote copies, remote signals or barrier semaphores. Data moves between devices by JAX's collectives and lax.ppermute only.
A program may use at most 64 MiB of HBM per device.

v0:
```python
import functools
import math

import jax
import jax.numpy as jnp
import numpy as np
from jax import lax
from jax.experimental import pallas as pl
from jax.experimental.pallas import tpu as pltpu
from jax.sharding import PartitionSpec as P

NF = 36
ND = 36
SIDE = 4
ROWS = 4
COLS = 128
CELLS = ROWS * COLS
BINS = NF * ND
FLAT = BINS * ROWS
PAD = 8
PIECES = SIDE**3
TOGETHER = 6
PIECE = FLAT // PIECES
TALL = 88
BLOCK = 72
GROUP = 3
CHUNK = 432
WIDTH = 512
UNIT = 512.0
STEPS = 65534.0
OFFSET = 32767
VMEM_BYTES = 24 * 1024 * 1024
SMALL_BYTES = 10 * 1024 * 1024
LARGE_BYTES = 56 * 1024 * 1024
STACK = 8

FRACTIONS = (0.25, 0.5, 0.75, 1.0)


def fraction(frac_index):
    open_share = jnp.zeros(frac_index.shape, jnp.float32)
    for position, share in enumerate(FRACTIONS):
        open_share = open_share + jnp.where(frac_index == position, share, 0.0)
    return open_share


def place(z, y, x):
    return (z % SIDE * SIDE + y % SIDE) * SIDE + x % SIDE


def hub_places():
    last = SIDE - 1
    return [
        place(last, last, last),
        place(last, last, last - 1),
        place(last, last - 1, last),
        place(last - 1, last, last),
    ]


def cube_member(cube, position):
    zyx = [2 * (cube // d % 2) + position // d % 2 for d in (4, 2, 1)]
    return (zyx[0] * SIDE + zyx[1]) * SIDE + zyx[2]


CUBES = 8
DIRECT = (6, 5, 3)
PASSED = (4, 1, 2, 0)
OWN = 7


def own_flags():
    return 1 - lax.axis_index("cell"), jnp.where(lax.axis_index("grid") == PIECES - 1, 0, 1)


def bin_block(ref, index):
    return ref[8 * index : 8 * index + 8, :]


def send_kernel(map_ref, spec_ref, maps_ref, *part_refs):
    lane = lax.broadcasted_iota(jnp.int32, (PIECES, COLS), 1)
    maps = jnp.zeros((PIECES, COLS), jnp.int32)
    for r in range(ROWS):
        for side in range(2):
            maps = jnp.where(lane == 2 * r + side, map_ref[side, r], maps)
    maps_ref[...] = maps
    part = FLAT // SIDE
    for k, ref in enumerate(part_refs):
        ref[...] = spec_ref[(k + 1) * part : (k + 2) * part, :]


def send_first(maps, spec):
    vmem = pl.BlockSpec(memory_space=pltpu.VMEM)
    part = jax.ShapeDtypeStruct((FLAT // SIDE, COLS), jnp.bfloat16)
    return pl.pallas_call(
        send_kernel,
        out_shape=(jax.ShapeDtypeStruct((PIECES, COLS), jnp.int32),) + (part,) * (SIDE - 1),
        in_specs=[pl.BlockSpec(memory_space=pltpu.SMEM), vmem],
        out_specs=(vmem,) * SIDE,
        compiler_params=pltpu.CompilerParams(vmem_limit_bytes=LARGE_BYTES),
    )(maps, spec)


def pick_kernel(maps_ref, spec_ref, a_ref, b_ref, c_ref, out_ref, wide, turned, hot, mine, sem):
    part = FLAT // SIDE
    bins = part // ROWS
    share = jnp.where(own_flags()[1] == 0, 1.0, 0.0)
    copy = pltpu.make_async_copy(spec_ref.at[pl.ds(0, part), :], mine, sem)
    copy.start()
    cell = lax.broadcasted_iota(jnp.int32, (PIECES, CELLS), 1)
    for e in range(2 * ROWS):
        wanted = jnp.broadcast_to(maps_ref[:, e : e + 1], (PIECES, CELLS))
        same = jnp.where(cell == wanted, 1.0, 0.0).astype(jnp.bfloat16)
        hot[e * PIECES : (e + 1) * PIECES, :] = same
    copy.wait()

    def join(i, carry):
        for u in range(9):
            at = pl.multiple_of(i * 144 + u * 16, 16)
            here = pl.ds(at, 16)
            value = mine[here, :].astype(jnp.float32) * share
            for ref in (a_ref, b_ref, c_ref):
                value = value + ref[here, :].astype(jnp.float32)
            wide[here, :] = value
        return carry

    lax.fori_loop(0, part // 144, join, 0)
    wide[part:, :] = jnp.zeros((wide.shape[0] - part, COLS), jnp.float32)
    many = wide.shape[0] // ROWS
    held = [wide[pl.ds(r, many, stride=ROWS), :].astype(jnp.bfloat16) for r in range(ROWS)]
    held = jnp.concatenate(held, axis=1)
    found = lax.dot_general(
        hot[...], held, (((1,), (1,)), ((), ())), preferred_element_type=jnp.float32
    )
    for e in range(2 * ROWS):
        for t in range(many // COLS):
            part = found[e * PIECES : (e + 1) * PIECES, t * COLS : (t + 1) * COLS]
            turned[t, pl.ds(e, PIECES, stride=2 * ROWS), :] = part

    def narrower(i, carry):
        for u in range(8):
            g = i * 8 + u
            at = pl.multiple_of(g * 2 * ROWS, 8)
            for t in range(many // COLS):
                lanes = min(COLS, bins - t * COLS)
                value = turned[t, pl.ds(at, 2 * ROWS), :lanes].astype(jnp.bfloat16)
                out_ref[g, :, t * COLS : t * COLS + lanes] = value
        return carry

    lax.fori_loop(0, PIECES // 8, narrower, 0)


def pick(*operands):
    vmem = pl.BlockSpec(memory_space=pltpu.VMEM)
    part = FLAT // SIDE
    return pl.pallas_call(
        pick_kernel,
        out_shape=jax.ShapeDtypeStruct((PIECES, 2 * ROWS, part // ROWS), jnp.bfloat16),
        in_specs=[vmem, pl.BlockSpec(memory_space=pl.ANY)] + [vmem] * 3,
        out_specs=vmem,
        scratch_shapes=[
            pltpu.VMEM((3 * COLS * ROWS, COLS), jnp.float32),
            pltpu.VMEM((3, PIECES * 2 * ROWS, COLS), jnp.float32),
            pltpu.VMEM((PIECES * 2 * ROWS, CELLS), jnp.bfloat16),
            pltpu.VMEM((part, COLS), jnp.bfloat16),
            pltpu.SemaphoreType.DMA,
        ],
        compiler_params=pltpu.CompilerParams(vmem_limit_bytes=SMALL_BYTES),
    )(*operands)


def prepare_kernel(spec_ref, depth_ref, wet_ref, frac_ref, near_ref, stat_ref, dens):
    first = own_flags()[0] == 1
    wet = wet_ref[...].astype(jnp.float32)
    values = (depth_ref[...], wet * fraction(frac_ref[...]), wet)
    for i, value in enumerate(values):
        stat_ref[2 * i : 2 * i + 1, :] = jnp.where(first, value[3:4], value[0:1])
        stat_ref[2 * i + 1 : 2 * i + 2, :] = jnp.where(first, value[2:3], value[1:2])
    stat_ref[6:8, :] = jnp.zeros((2, COLS), jnp.float32)

    def widen(i, carry):
        for u in range(12):
            at = pl.multiple_of(i * 192 + u * 16, 16)
            dens[pl.ds(at, 16), :] = spec_ref[pl.ds(at, 16), :].astype(jnp.float32)
        return carry

    lax.fori_loop(0, FLAT // 192, widen, 0)
    nearer = 3 * own_flags()[0]
    farther = 1 + own_flags()[0]

    def pull(i, carry):
        for u in range(9):
            at = pl.multiple_of(i * 144 + u * 16, 16)
            for n, row in enumerate((nearer, farther)):
                rows = dens[pl.ds(at * ROWS + row, 16, stride=ROWS), :]
                near_ref[n, pl.ds(at, 16), :] = rows.astype(jnp.bfloat16)
        return carry

    lax.fori_loop(0, BINS // 144, pull, 0)


def prepare(*operands, interpret=False):
    vmem = pl.BlockSpec(memory_space=pltpu.VMEM)
    return pl.pallas_call(
        prepare_kernel,
        out_shape=(
            jax.ShapeDtypeStruct((2, BINS, COLS), jnp.bfloat16),
            jax.ShapeDtypeStruct((8, COLS), jnp.float32),
        ),
        in_specs=[vmem] * 4,
        out_specs=(vmem,) * 2,
        scratch_shapes=[pltpu.VMEM((FLAT, COLS), jnp.float32)],
        compiler_params=pltpu.CompilerParams(vmem_limit_bytes=SMALL_BYTES),
        cost_estimate=pl.CostEstimate(flops=4_000_000, bytes_accessed=5_000_000, transcendentals=0),
        interpret=interpret,
    )(*operands)


def step_kernel(
    plus_ref,
    minus_ref,
    speed_ref,
    coef_ref,
    spec_ref,
    near_ref,
    edge_ref,
    far_ref,
    spot_ref,
    depth_ref,
    wet_ref,
    frac_ref,
    stat_ref,
    cos_ref,
    sin_ref,
    cosb_ref,
    sinb_ref,
    target_ref,
    out_ref,
    pieces_ref,
    dens,
    flat,
    halo,
    evol,
    near,
    hot,
    count,
    tab_x,
    tab_y,
    tab_z,
    tab_an,
    tab_nb,
    tab_n,
    done_out,
    out_sem,
):
    first = own_flags()[0] == 1
    child = own_flags()[1]
    adjacent = 3 * own_flags()[0]
    sign = jnp.where(first, 1.0, -1.0)
    lane = lax.broadcasted_iota(jnp.int32, (16, COLS), 1)
    ends = jnp.where((lane == 0) | (lane == COLS - 1), child, 0) > 0

    values = jnp.concatenate([edge_ref[...], far_ref[...]], axis=0)
    spot = spot_ref[1 - own_flags()[0]]
    for base in range(0, BINS, WIDTH):
        wide_rows = min(WIDTH, BINS - base)
        laid = lax.dot_general(
            values[:, base : base + wide_rows],
            spot,
            (((0,), (0,)), ((), ())),
            preferred_element_type=jnp.float32,
        )
        lanes = lax.broadcasted_iota(jnp.int32, (wide_rows, COLS), 1)
        ends_wide = jnp.where((lanes == 0) | (lanes == COLS - 1), child, 0) > 0
        for r in range(ROWS):
            here = pl.ds(base * ROWS + r, wide_rows, stride=ROWS)
            flat[here, :] = laid[:, r * COLS : (r + 1) * COLS]
        for n in range(2):
            raw = near_ref[n, base : base + wide_rows, :].astype(jnp.float32)
            at = (ROWS + n) * COLS
            raw = jnp.where(ends_wide, laid[:, at : at + COLS], raw)
            near[n, base : base + wide_rows, :] = raw * stat_ref[4 + n : 5 + n, :]

    wet = jnp.concatenate([wet_ref[...]] * 2, axis=0).astype(jnp.float32)
    wet16 = jnp.concatenate([wet, wet], axis=0)

    def begin(i, carry):
        for u in range(12):
            at = pl.multiple_of(i * 192 + u * 16, 16)
            raw = spec_ref[pl.ds(at, 16), :].astype(jnp.float32)
            dens[pl.ds(PAD + at, 16), :] = jnp.where(ends, flat[pl.ds(at, 16), :], raw) * wet16
            halo[pl.ds(at, 16), :] = jnp.zeros((16, COLS), jnp.float32)
        return carry

    lax.fori_loop(0, FLAT // 192, begin, 0)

    sub = lax.broadcasted_iota(jnp.int32, (8, COLS), 0)
    low = sub < ROWS
    depth = jnp.concatenate([depth_ref[...]] * 2, axis=0)
    weight = wet * fraction(jnp.concatenate([frac_ref[...]] * 2, axis=0))

    def between(d0, d1, w0, w1):
        return 0.5 * (d0 + d1) * w0 * w1

    def along(d, w):
        face = between(d, pltpu.roll(d, COLS - 1, 1), w, pltpu.roll(w, COLS - 1, 1))
        return jnp.where(lane[:8] == COLS - 1, 0.0, face)

    def wide(row):
        return jnp.broadcast_to(row, (8, COLS))

    face_x = between(depth, pltpu.roll(depth, 7, 0), weight, pltpu.roll(weight, 7, 0))
    face_x = jnp.where(sub % ROWS == ROWS - 1, 0.0, face_x)
    face_y = along(depth, weight)
    d_own = wide(jnp.where(first, depth[3:4], depth[0:1]))
    w_own = wide(jnp.where(first, weight[3:4], weight[0:1]))
    d_n1, d_n2, w_n1, w_n2 = (wide(stat_ref[i : i + 1, :]) for i in range(4))
    face_an = between(d_own, d_n1, w_own, w_n1)
    face_nb = between(d_n1, d_n2, w_n1, w_n2)
    face_n = along(d_n1, w_n1)

    for q in range(ND // 2):
        tab_x[8 * q : 8 * q + 8, :] = face_x * bin_block(cos_ref, q)
        tab_y[8 * q : 8 * q + 8, :] = face_y * bin_block(sin_ref, q)
        if 2 * q > ND // 2:
            back = 8 * (q - ND // 4)
            tab_z[back : back + 8, :] = pltpu.roll(face_y, 1, 1) * bin_block(sin_ref, q)
    for j in range(BLOCK // 8):
        tab_an[8 * j : 8 * j + 8, :] = face_an * bin_block(cosb_ref, j)
        tab_nb[8 * j : 8 * j + 8, :] = face_nb * bin_block(cosb_ref, j)
        tab_n[8 * j : 8 * j + 8, :] = face_n * bin_block(sinb_ref, j)

    def halo_fluxes(bins, rows):
        many = range(BLOCK // 8)
        n1s = [near[0, pl.ds(bins + 8 * j, 8), :] for j in many]
        owns = [dens[pl.ds(PAD + rows + 32 * j + adjacent, 8, stride=ROWS), :] for j in many]
        fluxes = []
        for j in many:
            along = bin_block(tab_an, j)
            top = jnp.where(first, owns[j], n1s[j])
            bottom = jnp.where(first, n1s[j], owns[j])
            fluxes.append(jnp.maximum(along, 0.0) * top + jnp.minimum(along, 0.0) * bottom)
        for j in many:
            halo[pl.ds(rows + 32 * j + adjacent, 8, stride=ROWS), :] = sign * fluxes[j]
        return n1s, fluxes

    def advance_near(bins, speeds, n1s, fluxes):
        n2s = [near[1, pl.ds(bins + 8 * j, 8), :] for j in range(BLOCK // 8)]
        after_near = []
        for j in range(BLOCK // 8):
            n1, n2 = n1s[j], n2s[j]
            top, bottom = jnp.where(first, n1, n2), jnp.where(first, n2, n1)
            along = bin_block(tab_nb, j)
            beyond = jnp.maximum(along, 0.0) * top + jnp.minimum(along, 0.0) * bottom
            along = bin_block(tab_n, j)
            right = pltpu.roll(n1, COLS - 1, 1)
            fy = jnp.maximum(along, 0.0) * n1 + jnp.minimum(along, 0.0) * right
            change = sign * (beyond - fluxes[j]) + (fy - pltpu.roll(fy, 1, 1))
            speed = speeds[0] if j < 4 else (jnp.where(low, *speeds) if j == 4 else speeds[1])
            after_near.append(n1 - speed * change)
        for j in range(BLOCK // 8):
            near[0, pl.ds(bins + 8 * j, 8), :] = after_near[j]

    def advance(q, speed, rho, across):
        along_x = bin_block(tab_x, q)
        if 2 * q + 1 < ND // 4 or 2 * q > 3 * ND // 4:
            fx = along_x * rho
        else:
            after = pltpu.roll(rho, 7, 0)
            if ND // 4 < 2 * q and 2 * q + 1 < 3 * ND // 4:
                fx = along_x * after
            else:
                fx = jnp.maximum(along_x, 0.0) * rho + jnp.minimum(along_x, 0.0) * after
        along_y = bin_block(tab_y, q)
        if 2 * q + 1 < ND // 2:
            fy = along_y * rho
            out_y = fy - pltpu.roll(fy, 1, 1)
        elif 2 * q > ND // 2:
            out_y = along_y * pltpu.roll(rho, COLS - 1, 1) - bin_block(tab_z, q - ND // 4) * rho
        else:
            right = pltpu.roll(rho, COLS - 1, 1)
            fy = jnp.maximum(along_y, 0.0) * rho + jnp.minimum(along_y, 0.0) * right
            out_y = fy - pltpu.roll(fy, 1, 1)
        change = (fx - pltpu.roll(fx, 1, 0)) + out_y
        return rho - speed * (change + across)

    def advance_all(starts, speeds):
        for q in range(0, ND // 2, GROUP):
            group = [
                (p, rows + 8 * (p + h * ND // 2), speed[h])
                for p in range(q, q + GROUP)
                for rows, speed in zip(starts, speeds)
                for h in range(2)
            ]
            loaded = [(dens[pl.ds(PAD + at, 8), :], halo[pl.ds(at, 8), :]) for _, at, _ in group]
            moved = [advance(p, speed, *pair) for (p, _, speed), pair in zip(group, loaded)]
            for (_, at, _), value in zip(group, moved):
                dens[pl.ds(PAD + at, 8), :] = value

    def blocks(i, carry):
        ks = [i * TOGETHER + u for u in range(TOGETHER)]
        bins = [pl.multiple_of(k * BLOCK, 8) for k in ks]
        rows = [pl.multiple_of(k * (BLOCK * ROWS), 16) for k in ks]
        speeds = [(speed_ref[2 * k], speed_ref[2 * k + 1]) for k in ks]
        halos = [halo_fluxes(*pair) for pair in zip(bins, rows)]
        for start, speed, values in zip(bins, speeds, halos):
            advance_near(start, speed, *values)
        advance_all(rows, speeds)
        for pair in zip(bins, rows):
            halo_fluxes(*pair)
        advance_all(rows, speeds)
        return carry

    lax.fori_loop(0, BINS // BLOCK // TOGETHER, blocks, 0)

    def interact(f, carry):
        rows = pl.multiple_of(f * (ND * ROWS), 16)
        scale = 0.2 * coef_ref[f]

        def partner(ref, b):
            lower = dens[pl.ds(ref[f * ND + b], 8), :]
            upper = dens[pl.ds(ref[f * ND + b + 1] - ROWS, 8), :]
            return jnp.where(low, lower, upper)

        for g in range(0, ND // 4, 3):
            bs = [4 * (g + t) + 2 * h for t in range(3) for h in range(2)]
            mines = [dens[pl.ds(PAD + rows + 4 * b, 8), :] for b in bs]
            pairs = [(partner(plus_ref, b), partner(minus_ref, b)) for b in bs]
            done = []
            for mine, (plus, minus) in zip(mines, pairs):
                source = mine * (mine * (plus + minus) - 2.0 * (plus * minus))
                done.append(jnp.maximum(mine + scale * source, 0.0))
            for b, value in zip(bs, done):
                evol[pl.ds(rows + 4 * b, 8), :] = value
            for t in range(3):
                both = jnp.concatenate(done[2 * t : 2 * t + 2], axis=0).astype(jnp.bfloat16)
                done_out[pl.ds(rows + 16 * (g + t), 16), :] = both
        return carry

    lax.fori_loop(0, NF, interact, 0)
    leaving = pltpu.make_async_copy(done_out, out_ref, out_sem)
    leaving.start()

    row = lax.broadcasted_iota(jnp.int32, (CELLS, COLS), 0)
    for r in range(ROWS):
        own = lane[:1] + r * COLS
        same = row == jnp.where(child == 1, target_ref[r : r + 1, :], own)
        hot[:, r * COLS : (r + 1) * COLS] = jnp.where(same, 1.0, 0.0).astype(jnp.bfloat16)
    inner = (((1,), (1,)), ((), ()))
    number = lax.dot_general(
        jnp.ones((16, CELLS), jnp.bfloat16), hot[...], inner, preferred_element_type=jnp.float32
    )
    share = 1.0 / jnp.maximum(number[0:1], 1.0)
    count[...] = jnp.zeros_like(count)
    for turn in range(ROWS):
        for r in range(ROWS):
            of = (turn + r) % ROWS
            here = number[0:1, of * COLS : (of + 1) * COLS].astype(jnp.int32)
            count[turn, PIECE % 8 + r : PIECE % 8 + r + 1, :] = here

    many = CHUNK

    def sums(c, carry):
        base = c * (many * ROWS)
        parts = [evol[pl.ds(base + r, many, stride=ROWS), :] for r in range(ROWS)]
        value = jnp.concatenate(parts, axis=1)
        head = value.astype(jnp.bfloat16)
        tail = (value - head.astype(jnp.float32)).astype(jnp.bfloat16)
        total = lax.dot_general(head, hot[...], inner, preferred_element_type=jnp.float32)
        total += lax.dot_general(tail, hot[...], inner, preferred_element_type=jnp.float32)
        for r in range(ROWS):
            part = slice(r * COLS, (r + 1) * COLS)
            flat[pl.ds(base + r, many, stride=ROWS), :] = total[:, part] * share[:, part]
        return carry

    lax.fori_loop(0, BINS // many, sums, 0)
    main = PIECE // 8 * 8
    row = main + lax.broadcasted_iota(jnp.int32, (8, COLS), 0)

    def cut(i, carry):
        for u in range(2 * ROWS):
            j, turn = i * 2 * ROWS + u, u % ROWS
            mean = flat[pl.ds(j * PIECE, main), :]
            last = jnp.where(row < PIECE, flat[pl.ds(j * PIECE + main, 8), :], 0.0)
            top = jnp.maximum(
                jnp.max(mean, axis=0, keepdims=True), jnp.max(last, axis=0, keepdims=True)
            )
            size = jnp.minimum((top * UNIT).astype(jnp.int32) + 1, OFFSET)
            steps = (UNIT * STEPS) / size.astype(jnp.float32)
            code = (mean * steps + 0.5).astype(jnp.int32) - OFFSET
            code_last = (last * steps + 0.5).astype(jnp.int32) - OFFSET
            rest = jnp.where(row == PIECE + ROWS, size, count[turn])
            code_last = jnp.where(row < PIECE, code_last, rest)
            code = jnp.concatenate([code, code_last], axis=0)
            pieces_ref[j] = code.astype(jnp.int16)
        return carry

    lax.fori_loop(0, PIECES // ROWS // 2, cut, 0)
    leaving.wait()


def evolve(*operands, interpret=False):
    smem = pl.BlockSpec(memory_space=pltpu.SMEM)
    vmem = pl.BlockSpec(memory_space=pltpu.VMEM)
    return pl.pallas_call(
        step_kernel,
        out_shape=(
            jax.ShapeDtypeStruct((FLAT, COLS), jnp.bfloat16),
            jax.ShapeDtypeStruct((PIECES, TALL, COLS), jnp.int16),
        ),
        in_specs=[smem] * 4 + [vmem] * 14,
        out_specs=(pl.BlockSpec(memory_space=pl.ANY), vmem),
        scratch_shapes=[
            pltpu.VMEM((FLAT + 2 * PAD, COLS), jnp.float32),
            pltpu.VMEM((FLAT + 2 * PAD, COLS), jnp.float32),
            pltpu.VMEM((FLAT, COLS), jnp.float32),
            pltpu.VMEM((FLAT, COLS), jnp.float32),
            pltpu.VMEM((2, BINS, COLS), jnp.float32),
            pltpu.VMEM((CELLS, CELLS), jnp.bfloat16),
            pltpu.VMEM((ROWS, 8, COLS), jnp.int32),
            pltpu.VMEM((ND * ROWS, COLS), jnp.float32),
            pltpu.VMEM((ND * ROWS, COLS), jnp.float32),
            pltpu.VMEM((ND * ROWS // 2, COLS), jnp.float32),
            pltpu.VMEM((BLOCK, COLS), jnp.float32),
            pltpu.VMEM((BLOCK, COLS), jnp.float32),
            pltpu.VMEM((BLOCK, COLS), jnp.float32),
            pltpu.VMEM((FLAT, COLS), jnp.bfloat16),
            pltpu.SemaphoreType.DMA,
        ],
        compiler_params=pltpu.CompilerParams(vmem_limit_bytes=VMEM_BYTES),
        cost_estimate=pl.CostEstimate(
            flops=1_400_000_000, bytes_accessed=10_000_000, transcendentals=0
        ),
        interpret=interpret,
    )(*operands)


def average_kernel(pieces_ref, out_ref):
    blocks = TALL // 8
    sub = lax.broadcasted_iota(jnp.int32, (8, COLS), 0)

    def add(i, carry):
        sums, weights, number = carry
        for u in range(4):
            piece = pieces_ref[4 * i + u].astype(jnp.int32).astype(jnp.float32)
            rest = piece[TALL - 8 :]
            at = PIECE % 8
            turned = [pltpu.roll(rest, shift - at, 0) for shift in (8, ROWS)]
            count = jnp.where(sub < ROWS, *turned)
            weight = count * jnp.broadcast_to(rest[at + ROWS : at + ROWS + 1], (8, COLS))
            sums = tuple(sums[b] + piece[8 * b : 8 * b + 8] * weight for b in range(blocks))
            weights, number = weights + weight, number + count
        return sums, weights, number

    zero = jnp.zeros((8, COLS), jnp.float32)
    carry = ((zero,) * blocks, zero, zero)
    sums, weights, number = lax.fori_loop(0, PIECES // 4, add, carry)
    scale = 1.0 / (UNIT * STEPS * number)
    mean = jnp.concatenate([(part + OFFSET * weights) * scale for part in sums], axis=0)
    mean = mean.astype(jnp.bfloat16)

    def write(i, carry):
        out_ref[i] = mean
        return carry

    lax.fori_loop(0, STACK, write, 0)


def average(pieces, interpret=False):
    vmem = pl.BlockSpec(memory_space=pltpu.VMEM)
    return pl.pallas_call(
        average_kernel,
        out_shape=jax.ShapeDtypeStruct((STACK, TALL, COLS), jnp.bfloat16),
        in_specs=[vmem],
        out_specs=vmem,
        compiler_params=pltpu.CompilerParams(vmem_limit_bytes=SMALL_BYTES),
        interpret=interpret,
    )(pieces)


def lay_kernel(*refs):
    parts, (_, out_ref, wide, narrow, sems) = refs[:CUBES], refs[CUBES:]
    main = PIECE // 8 * 8

    @pl.when(own_flags()[1] == 0)
    def _():
        for cube, ref in zip((OWN,) + DIRECT + PASSED, parts):
            for i in range(STACK):
                at = cube_member(cube, i) * PIECE
                piece = ref[i].astype(jnp.float32)
                wide[at : at + main, :] = piece[:main]
                wide[at + main : at + PIECE, :] = piece[main:PIECE]

        part = FLAT // SIDE
        copies = []
        for k in range(SIDE):

            def narrower(i, carry):
                for u in range(9):
                    at = pl.multiple_of(k * part + i * 144 + u * 16, 16)
                    narrow[pl.ds(at, 16), :] = wide[pl.ds(at, 16), :].astype(jnp.bfloat16)
                return carry

            lax.fori_loop(0, part // 144, narrower, 0)
            here = pl.ds(k * part, part)
            copies.append(pltpu.make_async_copy(narrow.at[here], out_ref.at[here], sems.at[k]))
            copies[k].start()
        for copy in copies:
            copy.wait()


def lay(parts, evolved):
    vmem = pl.BlockSpec(memory_space=pltpu.VMEM)
    anywhere = pl.BlockSpec(memory_space=pl.ANY)
    return pl.pallas_call(
        lay_kernel,
        out_shape=jax.ShapeDtypeStruct((FLAT, COLS), jnp.bfloat16),
        in_specs=[vmem] * CUBES + [anywhere],
        out_specs=anywhere,
        scratch_shapes=[
            pltpu.VMEM((FLAT + 2 * PAD, COLS), jnp.float32),
            pltpu.VMEM((FLAT, COLS), jnp.bfloat16),
            pltpu.SemaphoreType.DMA((SIDE,)),
        ],
        input_output_aliases={CUBES: 0},
        compiler_params=pltpu.CompilerParams(vmem_limit_bytes=SMALL_BYTES),
    )(*parts, evolved)


def tables():
    group_speed = 0.45 * np.exp(-math.log(1.1) * np.arange(NF))
    angles = 2.0 * math.pi / ND * np.arange(ND)

    def wide(values, times):
        return np.repeat(np.repeat(values, times)[:, None], COLS, axis=1).astype(np.float32)

    cosine, sine = np.cos(angles), np.sin(angles)
    twice = BLOCK // ND
    per_row = (wide(cosine, ROWS), wide(sine, ROWS))
    per_bin = (wide(np.tile(cosine, twice), 1), wide(np.tile(sine, twice), 1))
    return (group_speed.astype(np.float32),) + per_row + per_bin


def spots():
    both = []
    for cell in range(2):
        chosen = np.zeros((4 * ROWS, (ROWS + 2) * COLS), np.float32)
        near = (ROWS - 1, ROWS - 2) if cell else (0, 1)
        for block, source in enumerate(tuple(range(ROWS)) + tuple(ROWS + row for row in near)):
            chosen[2 * source, block * COLS] = 1.0
            chosen[2 * source + 1, (block + 1) * COLS - 1] = 1.0
        both.append(chosen)
    return np.stack(both).astype(jnp.bfloat16)


def swap(x):
    return lax.ppermute(x, "cell", [(0, 1), (1, 0)])


def on_device(
    spectrum,
    depth_factor,
    wet_mask,
    frac_index,
    boundary_map,
    average_map,
    dia_plus,
    dia_minus,
    dia_coef,
):
    parent = lax.axis_size("grid") - 1
    hubs = hub_places()
    spec = spectrum.reshape(FLAT, COLS)
    maps, *parts = send_first(boundary_map.T, spec)

    held = [lax.ppermute(part, "grid", [(parent, hub)]) for part, hub in zip(parts, hubs[1:])]
    maps = lax.all_to_all(maps, "grid", 0, 0)
    near, near_statics = prepare(spec, depth_factor, wet_mask, frac_index)
    near = swap(near)
    near_statics = swap(near_statics)
    picked = lax.all_to_all(pick(maps, spec, *held), "grid", 0, 0)
    picked = jnp.concatenate([picked[hub] for hub in hubs], axis=1)
    far = swap(picked)

    group_speed, cosine, sine, cosine_bin, sine_bin = tables()
    evolved, pieces = evolve(
        dia_plus * ROWS + PAD,
        dia_minus * ROWS + PAD,
        group_speed,
        dia_coef,
        spec,
        near,
        picked,
        far,
        spots(),
        depth_factor,
        wet_mask,
        frac_index,
        near_statics,
        cosine,
        sine,
        cosine_bin,
        sine_bin,
        average_map,
    )
    copies = average(lax.all_to_all(pieces, "grid", 0, 0))
    last = SIDE - 1
    cubes = [[cube_member(k, i) for i in range(STACK)] for k in range(CUBES)]
    gathered = lax.all_to_all(copies, "grid", 0, 0, axis_index_groups=cubes)
    wrapping = [place(last, last, 0), place(last, 0, last), place(0, last, last)]
    relays = [place(last, last, last - 1), place(last, last - 1, last), place(last - 1, last, last)]
    relays.append(wrapping[2])
    far = [place(last, 0, 1), place(0, 1, last), place(1, last, 0), place(0, 0, 0)]
    relayed = lax.ppermute(gathered, "grid", list(zip(far, relays)))
    parts = [lax.ppermute(gathered, "grid", [(device, parent)]) for device in wrapping]
    parts += [lax.ppermute(relayed, "grid", [(device, parent)]) for device in relays]
    parts = [gathered] + parts
    return lay(parts, evolved).reshape(BINS, ROWS, COLS)


def solution(mesh):
    placed = (
        P(None, ("grid", "cell"), None),
        P(("grid", "cell"), None),
        P(("grid", "cell"), None),
        P(("grid", "cell"), None),
        P(("grid", "cell"), None),
        P(("grid", "cell"), None),
        P(),
        P(),
        P(),
    )
    return jax.shard_map(
        on_device,
        mesh=mesh,
        in_specs=placed,
        out_specs=P(None, ("grid", "cell"), None),
        check_vma=False,
    )
```

profile of v0, /device:TPU:126, one launch (start us, length us, event | category | flops | bytes accessed | tf_op | source)
XLA Modules:
  0.0 107.7 jit_solution(17199205178553069776)
XLA Ops:
  0.0 2.4 %shard_map.146 = (s32[64,128]{1,0:T(8,128)}, bf16[1296,128]{1,0:T(8,128)(2,1)}, bf16[1296,128]{1,0:T(8,128)(2,1)}, bf16[1296,128]{1,0:T(8,128)(2,1)}) custom-call(s32[2,4]{1,0:T(2,128)} %bitcast.21, bf16[5184,128]{1,0:T(8,128)(2,1)} %bitcast.15), custom_call_target="tpu_custom_call" | custom-call | tf_op jit(solution)/shard_map/pallas_call | solution.py:95
  2.4 2.7 %collective-permute-start.1 = (bf16[1296,128]{1,0:T(8,128)(2,1)}, bf16[1296,128]{1,0:T(8,128)(2,1)S(1)}, u32[]{:S(2)}, u32[]{:S(2)}) collective-permute-start(bf16[1296,128]{1,0:T(8,128)(2,1)} %get-tuple-element.15), channel_id=1, source_target_pairs={{126,124},{127,125}} | collective-permute-start | bytes 995336 | tf_op jit(solution)/shard_map/ppermute | solution.py:676
  5.2 1.3 %collective-permute-start.2 = (bf16[1296,128]{1,0:T(8,128)(2,1)}, bf16[1296,128]{1,0:T(8,128)(2,1)S(1)}, u32[]{:S(2)}, u32[]{:S(2)}) collective-permute-start(bf16[1296,128]{1,0:T(8,128)(2,1)} %get-tuple-element.16), channel_id=1, source_target_pairs={{126,118},{127,119}} | collective-permute-start | bytes 995336 | tf_op jit(solution)/shard_map/ppermute | solution.py:676
  6.5 1.3 %collective-permute-start.3 = (bf16[1296,128]{1,0:T(8,128)(2,1)}, bf16[1296,128]{1,0:T(8,128)(2,1)S(1)}, u32[]{:S(2)}, u32[]{:S(2)}) collective-permute-start(bf16[1296,128]{1,0:T(8,128)(2,1)} %get-tuple-element.17), channel_id=1, source_target_pairs={{126,94},{127,95}} | collective-permute-start | bytes 995336 | tf_op jit(solution)/shard_map/ppermute | solution.py:676
  7.8 14.2 %all_to_all.26 = s32[64,1,128]{2,1,0:T(1,128)S(1)} all-to-all(s32[64,1,128]{2,1,0:T(1,128)} %bitcast.20), channel_id=1, replica_groups=mesh['grid'=64,'cell'=2] {'grid'}, dimensions={0} | all-to-all | bytes 65536 | tf_op jit(solution)/shard_map/all_to_all | solution.py:677
  22.0 0.0 collective-permute-done.1.a_ref
  22.0 0.0 collective-permute-done.2.b_ref
  22.0 0.0 copy-start.1
  22.0 0.0 copy-start.2
  22.0 0.0 copy-start.3
  22.0 1.8 %shard_map.147 = bf16[64,8,324]{2,1,0:T(8,128)(2,1)} custom-call(s32[64,128]{1,0:T(8,128)S(1)} %bitcast.19, bf16[5184,128]{1,0:T(8,128)(2,1)S(1)} %bitcast.16, bf16[1296,128]{1,0:T(8,128)(2,1)S(1)} %collective-permute-done.1.a_ref, bf16[1296,128]{1,0:T(8,128)(2,1)S(1)} %collective-permute-done.2.b_ref, bf16[1296,128]{1,0:T(8,128)(2,1)S(1)} %collective-permute-done.3.c_ref), custom_call_target="tpu_custom_call" | custom-call | tf_op jit(solution)/shard_map/pallas_call | solution.py:156
  23.9 0.0 copy-start.12
  23.9 0.0 copy-start.13
  23.9 0.0 copy-start.4
  23.9 0.0 copy-start.5
  23.9 0.0 copy-start.6
  23.9 0.0 copy-start.7
  23.9 0.0 copy-start.8
  24.0 0.0 copy-start.9
  24.0 0.0 copy-start.10
  24.0 0.0 copy-start.11
  24.0 10.1 %all-to-all-start.1 = ((bf16[64,8,324]{2,1,0:T(8,128)(2,1)}), bf16[64,8,324]{2,1,0:T(8,128)(2,1)S(1)}, u32[]{:S(2)}, u32[]{:S(2)}) async-start(bf16[64,8,324]{2,1,0:T(8,128)(2,1)} %shard_map.147), calls=%async_computation.1 | async-start | bytes 786432 | tf_op jit(solution)/shard_map/all_to_all | solution.py:681
  34.1 0.7 shard_map.145
  34.8 0.1 collective-permute-start
  34.9 0.5 collective-permute-start.5
  35.4 4.7 %all-to-all-done.1 = bf16[64,8,324]{2,1,0:T(8,128)(2,1)S(1)} async-done(((bf16[64,8,324]{2,1,0:T(8,128)(2,1)}), bf16[64,8,324]{2,1,0:T(8,128)(2,1)S(1)}, u32[]{:S(2)}, u32[]{:S(2)}) %all-to-all-start.1) | async-done | bytes 331808 | tf_op jit(solution)/shard_map/all_to_all | solution.py:681
  40.1 0.1 concatenate.3.edge_ref
  40.2 0.1 collective-permute-start.4
  40.3 0.0 collective-permute-done.5.stat_ref
  40.3 0.0 collective-permute-done.near_ref
  40.3 1.1 %collective-permute-done.4.far_ref = bf16[8,1296]{1,0:T(8,128)(2,1)S(1)} collective-permute-done((bf16[8,1296]{1,0:T(8,128)(2,1)S(1)}, bf16[8,1296]{1,0:T(8,128)(2,1)S(1)}, u32[]{:S(2)}, u32[]{:S(2)}) %collective-permute-start.4) | collective-permute-done | bytes 20768 | tf_op jit(solution)/shard_map/ppermute | solution.py:657
  41.5 10.7 %shard_map.148 = (bf16[5184,128]{1,0:T(8,128)(2,1)}, s16[64,88,128]{2,1,0:T(8,128)(2,1)S(1)}) custom-call(s32[1296]{0:T(1024)S(1)} %get-tuple-element.26.plus_ref, s32[1296]{0:T(1024)S(1)} %get-tuple-element.25.minus_ref, f32[36]{0:T(128)S(1)} %copy-done.11, f32[36]{0:T(128)S(1)} %copy-done.5, bf16[5184,128]{1,0:T(8,128)(2,1)S(1)} %bitcast.18, ...), custom_call_target="tpu_custom_call" | custom-call | flops 1400000000 | bytes 10000000 | tf_op jit(solution)/shard_map/pallas_call | solution.py:505
  52.3 27.1 %all_to_all.27.pieces_ref = s16[64,88,128]{2,1,0:T(8,128)(2,1)S(1)} all-to-all(s16[64,88,128]{2,1,0:T(8,128)(2,1)S(1)} %get-tuple-element.19), channel_id=1, replica_groups=mesh['grid'=64,'cell'=2] {'grid'}, dimensions={0} | all-to-all | bytes 2883584 | tf_op jit(solution)/shard_map/all_to_all | solution.py:706
  79.4 0.5 shard_map.149
  79.9 8.4 %all_to_all.28.refs_0_ = bf16[8,88,128]{2,1,0:T(8,128)(2,1)S(1)} all-to-all(bf16[8,88,128]{2,1,0:T(8,128)(2,1)S(1)} %shard_map.149), channel_id=1, replica_groups={{0,2,8,10,32,34,40,42},{4,6,12,14,36,38,44,46},{16,18,24,26,48,50,56,58..., dimensions={0} | all-to-all | bytes 360448 | tf_op jit(solution)/shard_map/all_to_all | solution.py:709
  88.3 0.7 collective-permute-start.9
  89.0 1.3 %collective-permute-start.8 = (bf16[8,88,128]{2,1,0:T(8,128)(2,1)S(1)}, bf16[8,88,128]{2,1,0:T(8,128)(2,1)S(1)}, u32[]{:S(2)}, u32[]{:S(2)}) collective-permute-start(bf16[8,88,128]{2,1,0:T(8,128)(2,1)S(1)} %all_to_all.28.refs_0_), channel_id=1, source_target_pairs={{30,126},{31,127}} | collective-permute-start | bytes 540680 | tf_op jit(solution)/shard_map/ppermute | solution.py:715
  90.3 1.3 %collective-permute-start.7 = (bf16[8,88,128]{2,1,0:T(8,128)(2,1)S(1)}, bf16[8,88,128]{2,1,0:T(8,128)(2,1)S(1)}, u32[]{:S(2)}, u32[]{:S(2)}) collective-permute-start(bf16[8,88,128]{2,1,0:T(8,128)(2,1)S(1)} %all_to_all.28.refs_0_), channel_id=1, source_target_pairs={{102,126},{103,127}} | collective-permute-start | bytes 540680 | tf_op jit(solution)/shard_map/ppermute | solution.py:715
  91.6 1.3 %collective-permute-start.6 = (bf16[8,88,128]{2,1,0:T(8,128)(2,1)S(1)}, bf16[8,88,128]{2,1,0:T(8,128)(2,1)S(1)}, u32[]{:S(2)}, u32[]{:S(2)}) collective-permute-start(bf16[8,88,128]{2,1,0:T(8,128)(2,1)S(1)} %all_to_all.28.refs_0_), channel_id=1, source_target_pairs={{120,126},{121,127}} | collective-permute-start | bytes 540680 | tf_op jit(solution)/shard_map/ppermute | solution.py:715
  92.9 1.3 %collective-permute-start.13 = (bf16[8,88,128]{2,1,0:T(8,128)(2,1)S(1)}, bf16[8,88,128]{2,1,0:T(8,128)(2,1)S(1)}, u32[]{:S(2)}, u32[]{:S(2)}) collective-permute-start(bf16[8,88,128]{2,1,0:T(8,128)(2,1)S(1)} %collective-permute-done.9), channel_id=1, source_target_pairs={{30,126},{31,127}} | collective-permute-start | bytes 540680 | tf_op jit(solution)/shard_map/ppermute | solution.py:716
  94.2 1.3 %collective-permute-start.12 = (bf16[8,88,128]{2,1,0:T(8,128)(2,1)S(1)}, bf16[8,88,128]{2,1,0:T(8,128)(2,1)S(1)}, u32[]{:S(2)}, u32[]{:S(2)}) collective-permute-start(bf16[8,88,128]{2,1,0:T(8,128)(2,1)S(1)} %collective-permute-done.9), channel_id=1, source_target_pairs={{94,126},{95,127}} | collective-permute-start | bytes 540680 | tf_op jit(solution)/shard_map/ppermute | solution.py:716
  95.5 2.1 %collective-permute-done.8.refs_3_ = bf16[8,88,128]{2,1,0:T(8,128)(2,1)S(1)} collective-permute-done((bf16[8,88,128]{2,1,0:T(8,128)(2,1)S(1)}, bf16[8,88,128]{2,1,0:T(8,128)(2,1)S(1)}, u32[]{:S(2)}, u32[]{:S(2)}) %collective-permute-start.8) | collective-permute-done | bytes 180256 | tf_op jit(solution)/shard_map/ppermute | solution.py:715
  97.6 1.3 %collective-permute-start.11 = (bf16[8,88,128]{2,1,0:T(8,128)(2,1)S(1)}, bf16[8,88,128]{2,1,0:T(8,128)(2,1)S(1)}, u32[]{:S(2)}, u32[]{:S(2)}) collective-permute-start(bf16[8,88,128]{2,1,0:T(8,128)(2,1)S(1)} %collective-permute-done.9), channel_id=1, source_target_pairs={{118,126},{119,127}} | collective-permute-start | bytes 540680 | tf_op jit(solution)/shard_map/ppermute | solution.py:716
  98.9 0.0 collective-permute-done.7.refs_2_
  98.9 1.3 %collective-permute-start.10 = (bf16[8,88,128]{2,1,0:T(8,128)(2,1)S(1)}, bf16[8,88,128]{2,1,0:T(8,128)(2,1)S(1)}, u32[]{:S(2)}, u32[]{:S(2)}) collective-permute-start(bf16[8,88,128]{2,1,0:T(8,128)(2,1)S(1)} %collective-permute-done.9), channel_id=1, source_target_pairs={{124,126},{125,127}} | collective-permute-start | bytes 540680 | tf_op jit(solution)/shard_map/ppermute | solution.py:716
  100.2 5.8 %collective-permute-done.13.refs_7_ = bf16[8,88,128]{2,1,0:T(8,128)(2,1)S(1)} collective-permute-done((bf16[8,88,128]{2,1,0:T(8,128)(2,1)S(1)}, bf16[8,88,128]{2,1,0:T(8,128)(2,1)S(1)}, u32[]{:S(2)}, u32[]{:S(2)}) %collective-permute-start.13) | collective-permute-done | bytes 180256 | tf_op jit(solution)/shard_map/ppermute | solution.py:716
  106.0 0.3 collective-permute-done.10.refs_4_
  106.3 1.4 %shard_map.150 = bf16[5184,128]{1,0:T(8,128)(2,1)} custom-call(bf16[8,88,128]{2,1,0:T(8,128)(2,1)S(1)} %all_to_all.28.refs_0_, bf16[8,88,128]{2,1,0:T(8,128)(2,1)S(1)} %collective-permute-done.6.refs_1_, bf16[8,88,128]{2,1,0:T(8,128)(2,1)S(1)} %collective-permute-done.7.refs_2_, ...), custom_call_target="tpu_custom_call", output_to_operand_aliasing={{}: (8, {})} | custom-call | tf_op jit(solution)/shard_map/pallas_call | solution.py:615
  (22 shorter events, 0.1 us)
Async XLA Ops:
  0.0 22.0 %copy-start = (bf16[1296,4,128]{2,1,0:T(4,128)(2,1)S(1)}, bf16[1296,4,128]{2,1,0:T(4,128)(2,1)}, u32[]{:S(2)}) copy-start(bf16[1296,4,128]{2,1,0:T(4,128)(2,1)} %param.15) | copy-start | bytes 3981316
  2.4 19.6 %collective-permute-start.1 = (bf16[1296,128]{1,0:T(8,128)(2,1)}, bf16[1296,128]{1,0:T(8,128)(2,1)S(1)}, u32[]{:S(2)}, u32[]{:S(2)}) collective-permute-start(bf16[1296,128]{1,0:T(8,128)(2,1)} %get-tuple-element.15), channel_id=1, source_target_pairs={{126,124},{127,125}} | collective-permute-start | bytes 995336 | tf_op jit(solution)/shard_map/ppermute | solution.py:676
  5.2 16.8 %collective-permute-start.2 = (bf16[1296,128]{1,0:T(8,128)(2,1)}, bf16[1296,128]{1,0:T(8,128)(2,1)S(1)}, u32[]{:S(2)}, u32[]{:S(2)}) collective-permute-start(bf16[1296,128]{1,0:T(8,128)(2,1)} %get-tuple-element.16), channel_id=1, source_target_pairs={{126,118},{127,119}} | collective-permute-start | bytes 995336 | tf_op jit(solution)/shard_map/ppermute | solution.py:676
  6.5 15.5 %collective-permute-start.3 = (bf16[1296,128]{1,0:T(8,128)(2,1)}, bf16[1296,128]{1,0:T(8,128)(2,1)S(1)}, u32[]{:S(2)}, u32[]{:S(2)}) collective-permute-start(bf16[1296,128]{1,0:T(8,128)(2,1)} %get-tuple-element.17), channel_id=1, source_target_pairs={{126,94},{127,95}} | collective-permute-start | bytes 995336 | tf_op jit(solution)/shard_map/ppermute | solution.py:676
  22.0 12.1 %copy-start.1 = (f32[4,128]{1,0:T(4,128)S(1)}, f32[4,128]{1,0:T(4,128)}, u32[]{:S(2)}) copy-start(f32[4,128]{1,0:T(4,128)} %depth_ref.3) | copy-start | bytes 6148
  22.0 12.1 %copy-start.2 = (s32[4,128]{1,0:T(4,128)S(1)}, s32[4,128]{1,0:T(4,128)}, u32[]{:S(2)}) copy-start(s32[4,128]{1,0:T(4,128)} %wet_ref.3) | copy-start | bytes 6148
  22.0 12.1 %copy-start.3 = (s32[4,128]{1,0:T(4,128)S(1)}, s32[4,128]{1,0:T(4,128)}, u32[]{:S(2)}) copy-start(s32[4,128]{1,0:T(4,128)} %frac_ref.3) | copy-start | bytes 6148
  23.9 16.4 %copy-start.12 = (s32[1296]{0:T(1024)S(1)}, s32[1296]{0:T(1024)}, u32[]{:S(2)}) copy-start(s32[1296]{0:T(1024)} %param.22) | copy-start | bytes 15556
  23.9 16.4 %copy-start.13 = (s32[1296]{0:T(1024)S(1)}, s32[1296]{0:T(1024)}, u32[]{:S(2)}) copy-start(s32[1296]{0:T(1024)} %param.21) | copy-start | bytes 15556
  23.9 17.6 %copy-start.4 = (s32[4,128]{1,0:T(4,128)S(1)}, s32[4,128]{1,0:T(4,128)}, u32[]{:S(2)}) copy-start(s32[4,128]{1,0:T(4,128)} %target_ref.1) | copy-start | bytes 6148
  23.9 17.6 %copy-start.5 = (f32[36]{0:T(128)S(1)}, f32[36]{0:T(128)}, u32[]{:S(2)}) copy-start(f32[36]{0:T(128)} %coef_ref.1) | copy-start | bytes 436
  23.9 17.6 %copy-start.6 = (f32[144,128]{1,0:T(8,128)S(1)}, f32[144,128]{1,0:T(8,128)}, u32[]{:S(2)}) copy-start(f32[144,128]{1,0:T(8,128)} %constant.19.clone.sin_ref) | copy-start | bytes 221188
  23.9 17.5 %copy-start.7 = (f32[144,128]{1,0:T(8,128)S(1)}, f32[144,128]{1,0:T(8,128)}, u32[]{:S(2)}) copy-start(f32[144,128]{1,0:T(8,128)} %constant.18.clone.cos_ref) | copy-start | bytes 221188
  23.9 17.5 %copy-start.8 = (bf16[2,16,768]{2,1,0:T(8,128)(2,1)S(1)}, bf16[2,16,768]{2,1,0:T(8,128)(2,1)}, u32[]{:S(2)}) copy-start(bf16[2,16,768]{2,1,0:T(8,128)(2,1)} %constant.17.clone.spot_ref) | copy-start | bytes 147460
  24.0 17.5 %copy-start.9 = (f32[72,128]{1,0:T(8,128)S(1)}, f32[72,128]{1,0:T(8,128)}, u32[]{:S(2)}) copy-start(f32[72,128]{1,0:T(8,128)} %constant.21.clone.sinb_ref) | copy-start | bytes 110596
  24.0 17.5 %copy-start.10 = (f32[72,128]{1,0:T(8,128)S(1)}, f32[72,128]{1,0:T(8,128)}, u32[]{:S(2)}) copy-start(f32[72,128]{1,0:T(8,128)} %constant.20.clone.cosb_ref) | copy-start | bytes 110596
  24.0 17.5 %copy-start.11 = (f32[36]{0:T(128)S(1)}, f32[36]{0:T(128)}, u32[]{:S(2)}) copy-start(f32[36]{0:T(128)} %constant.16.clone.speed_ref) | copy-start | bytes 436
  24.0 16.1 %all-to-all-start.1 = ((bf16[64,8,324]{2,1,0:T(8,128)(2,1)}), bf16[64,8,324]{2,1,0:T(8,128)(2,1)S(1)}, u32[]{:S(2)}, u32[]{:S(2)}) async-start(bf16[64,8,324]{2,1,0:T(8,128)(2,1)} %shard_map.147), calls=%async_computation.1 | async-start | bytes 786432 | tf_op jit(solution)/shard_map/all_to_all | solution.py:681
  34.8 5.5 %collective-permute-start = (bf16[2,1296,128]{2,1,0:T(8,128)(2,1)S(1)}, bf16[2,1296,128]{2,1,0:T(8,128)(2,1)S(1)}, u32[]{:S(2)}, u32[]{:S(2)}) collective-permute-start(bf16[2,1296,128]{2,1,0:T(8,128)(2,1)S(1)} %get-tuple-element.13), channel_id=1, source_target_pairs={{0,1},{1,0},{2,3},{3,2},{4,5},{5,4},{6,7},{7,6},{8,9},{9,8},{10,11... | collective-permute-start | bytes 1990664 | tf_op jit(solution)/shard_map/ppermute | solution.py:657
  34.9 5.4 %collective-permute-start.5 = (f32[8,128]{1,0:T(8,128)S(1)}, f32[8,128]{1,0:T(8,128)S(1)}, u32[]{:S(2)}, u32[]{:S(2)}) collective-permute-start(f32[8,128]{1,0:T(8,128)S(1)} %get-tuple-element.18), channel_id=1, source_target_pairs={{0,1},{1,0},{2,3},{3,2},{4,5},{5,4},{6,7},{7,6},{8,9},{9,8},{10,11... | collective-permute-start | bytes 12296 | tf_op jit(solution)/shard_map/ppermute | solution.py:657
  40.2 1.3 %collective-permute-start.4 = (bf16[8,1296]{1,0:T(8,128)(2,1)S(1)}, bf16[8,1296]{1,0:T(8,128)(2,1)S(1)}, u32[]{:S(2)}, u32[]{:S(2)}) collective-permute-start(bf16[8,1296]{1,0:T(8,128)(2,1)S(1)} %concatenate.3.edge_ref), channel_id=1, source_target_pairs={{0,1},{1,0},{2,3},{3,2},{4,5},{5,4},{6,7},{7,6},{8,9},{9,8},{10,11... | collective-permute-start | bytes 62216 | tf_op jit(solution)/shard_map/ppermute | solution.py:657
  88.3 4.6 %collective-permute-start.9 = (bf16[8,88,128]{2,1,0:T(8,128)(2,1)S(1)}, bf16[8,88,128]{2,1,0:T(8,128)(2,1)S(1)}, u32[]{:S(2)}, u32[]{:S(2)}) collective-permute-start(bf16[8,88,128]{2,1,0:T(8,128)(2,1)S(1)} %all_to_all.28.refs_0_), channel_id=1, source_target_pairs={{98,124},{14,118},{56,94},{0,30},{99,125},{15,119},{57,95},{1,31}} | collective-permute-start | bytes 540680 | tf_op jit(solution)/shard_map/ppermute | solution.py:714
  89.0 8.6 %collective-permute-start.8 = (bf16[8,88,128]{2,1,0:T(8,128)(2,1)S(1)}, bf16[8,88,128]{2,1,0:T(8,128)(2,1)S(1)}, u32[]{:S(2)}, u32[]{:S(2)}) collective-permute-start(bf16[8,88,128]{2,1,0:T(8,128)(2,1)S(1)} %all_to_all.28.refs_0_), channel_id=1, source_target_pairs={{30,126},{31,127}} | collective-permute-start | bytes 540680 | tf_op jit(solution)/shard_map/ppermute | solution.py:715
  90.3 8.6 %collective-permute-start.7 = (bf16[8,88,128]{2,1,0:T(8,128)(2,1)S(1)}, bf16[8,88,128]{2,1,0:T(8,128)(2,1)S(1)}, u32[]{:S(2)}, u32[]{:S(2)}) collective-permute-start(bf16[8,88,128]{2,1,0:T(8,128)(2,1)S(1)} %all_to_all.28.refs_0_), channel_id=1, source_target_pairs={{102,126},{103,127}} | collective-permute-start | bytes 540680 | tf_op jit(solution)/shard_map/ppermute | solution.py:715
  91.6 8.6 %collective-permute-start.6 = (bf16[8,88,128]{2,1,0:T(8,128)(2,1)S(1)}, bf16[8,88,128]{2,1,0:T(8,128)(2,1)S(1)}, u32[]{:S(2)}, u32[]{:S(2)}) collective-permute-start(bf16[8,88,128]{2,1,0:T(8,128)(2,1)S(1)} %all_to_all.28.refs_0_), channel_id=1, source_target_pairs={{120,126},{121,127}} | collective-permute-start | bytes 540680 | tf_op jit(solution)/shard_map/ppermute | solution.py:715
  92.9 13.1 %collective-permute-start.13 = (bf16[8,88,128]{2,1,0:T(8,128)(2,1)S(1)}, bf16[8,88,128]{2,1,0:T(8,128)(2,1)S(1)}, u32[]{:S(2)}, u32[]{:S(2)}) collective-permute-start(bf16[8,88,128]{2,1,0:T(8,128)(2,1)S(1)} %collective-permute-done.9), channel_id=1, source_target_pairs={{30,126},{31,127}} | collective-permute-start | bytes 540680 | tf_op jit(solution)/shard_map/ppermute | solution.py:716
  94.2 11.8 %collective-permute-start.12 = (bf16[8,88,128]{2,1,0:T(8,128)(2,1)S(1)}, bf16[8,88,128]{2,1,0:T(8,128)(2,1)S(1)}, u32[]{:S(2)}, u32[]{:S(2)}) collective-permute-start(bf16[8,88,128]{2,1,0:T(8,128)(2,1)S(1)} %collective-permute-done.9), channel_id=1, source_target_pairs={{94,126},{95,127}} | collective-permute-start | bytes 540680 | tf_op jit(solution)/shard_map/ppermute | solution.py:716
  97.6 8.4 %collective-permute-start.11 = (bf16[8,88,128]{2,1,0:T(8,128)(2,1)S(1)}, bf16[8,88,128]{2,1,0:T(8,128)(2,1)S(1)}, u32[]{:S(2)}, u32[]{:S(2)}) collective-permute-start(bf16[8,88,128]{2,1,0:T(8,128)(2,1)S(1)} %collective-permute-done.9), channel_id=1, source_target_pairs={{118,126},{119,127}} | collective-permute-start | bytes 540680 | tf_op jit(solution)/shard_map/ppermute | solution.py:716
  98.9 7.4 %collective-permute-start.10 = (bf16[8,88,128]{2,1,0:T(8,128)(2,1)S(1)}, bf16[8,88,128]{2,1,0:T(8,128)(2,1)S(1)}, u32[]{:S(2)}, u32[]{:S(2)}) collective-permute-start(bf16[8,88,128]{2,1,0:T(8,128)(2,1)S(1)} %collective-permute-done.9), channel_id=1, source_target_pairs={{124,126},{125,127}} | collective-permute-start | bytes 540680 | tf_op jit(solution)/shard_map/ppermute | solution.py:716
where the time goes:
time: 108 us
  blocking collectives  49.7 us (46%)
  starting transfers between devices  25.8 us (24%)
  Pallas kernels  17.6 us (16%)
  waiting for transfers between devices  14 us (13%)
    all_to_all x1, blocking collectives, on_device(): copies = average(lax.all_to_all(pieces, 'grid', 0, 0))  27.1 us
    all_to_all x1, blocking collectives, on_device(): maps = lax.all_to_all(maps, 'grid', 0, 0)  14.2 us
    pallas_call x1, Pallas kernels, evolve(): pl.pallas_call(step_kernel, out_shape=(jax.ShapeDtypeStruct((FLAT, COLS),...  10.7 us
    all_to_all x1, starting transfers between devices, on_device(): picked = lax.all_to_all(pick(maps, spec, *held), 'grid', 0, 0)  10.1 us
    all_to_all x1, blocking collectives, on_device(): gathered = lax.all_to_all(copies, 'grid', 0, 0, axis_index_groups=cubes)  8.39 us
    ppermute x4, waiting for transfers between devices, on_device(): lax.ppermute(relayed, 'grid', [(device, parent)])  6.08 us
    ppermute x3, starting transfers between devices, on_device(): lax.ppermute(part, 'grid', [(parent, hub)])  5.36 us
    ppermute x4, starting transfers between devices, on_device(): lax.ppermute(relayed, 'grid', [(device, parent)])  5.16 us
  transfers between devices with their start and end apart: 15, of which 5 were waited for; matrix products, arithmetic and copies ran while one was open for 0% of the time, Pallas kernels for 1%

commit v1 on v0

--- a/solution.py
+++ b/solution.py
@@ -33,6 +33,7 @@
 SMALL_BYTES = 10 * 1024 * 1024
 LARGE_BYTES = 56 * 1024 * 1024
 STACK = 8
+HELD = 384
 
 FRACTIONS = (0.25, 0.5, 0.75, 1.0)
 
@@ -101,17 +102,11 @@
     )(maps, spec)
 
 
-def pick_kernel(maps_ref, spec_ref, a_ref, b_ref, c_ref, out_ref, wide, turned, hot, mine, sem):
+def join_kernel(spec_ref, a_ref, b_ref, c_ref, out_ref, wide, mine, sem):
     part = FLAT // SIDE
-    bins = part // ROWS
     share = jnp.where(own_flags()[1] == 0, 1.0, 0.0)
     copy = pltpu.make_async_copy(spec_ref.at[pl.ds(0, part), :], mine, sem)
     copy.start()
-    cell = lax.broadcasted_iota(jnp.int32, (PIECES, CELLS), 1)
-    for e in range(2 * ROWS):
-        wanted = jnp.broadcast_to(maps_ref[:, e : e + 1], (PIECES, CELLS))
-        same = jnp.where(cell == wanted, 1.0, 0.0).astype(jnp.bfloat16)
-        hot[e * PIECES : (e + 1) * PIECES, :] = same
     copy.wait()
 
     def join(i, carry):
@@ -127,13 +122,41 @@
     lax.fori_loop(0, part // 144, join, 0)
     wide[part:, :] = jnp.zeros((wide.shape[0] - part, COLS), jnp.float32)
     many = wide.shape[0] // ROWS
-    held = [wide[pl.ds(r, many, stride=ROWS), :].astype(jnp.bfloat16) for r in range(ROWS)]
-    held = jnp.concatenate(held, axis=1)
+    for r in range(ROWS):
+        row = wide[pl.ds(r, many, stride=ROWS), :].astype(jnp.bfloat16)
+        out_ref[:, r * COLS : (r + 1) * COLS] = row
+
+
+def join_held(*operands):
+    vmem = pl.BlockSpec(memory_space=pltpu.VMEM)
+    part = FLAT // SIDE
+    return pl.pallas_call(
+        join_kernel,
+        out_shape=jax.ShapeDtypeStruct((HELD, CELLS), jnp.bfloat16),
+        in_specs=[pl.BlockSpec(memory_space=pl.ANY)] + [vmem] * 3,
+        out_specs=vmem,
+        scratch_shapes=[
+            pltpu.VMEM((HELD * ROWS, COLS), jnp.float32),
+            pltpu.VMEM((part, COLS), jnp.bfloat16),
+            pltpu.SemaphoreType.DMA,
+        ],
+        compiler_params=pltpu.CompilerParams(vmem_limit_bytes=SMALL_BYTES),
+        cost_estimate=pl.CostEstimate(flops=2_000_000, bytes_accessed=2_000_000, transcendentals=0),
+    )(*operands)
+
+
+def pick_kernel(maps_ref, held_ref, out_ref, turned, hot):
+    bins = BINS // SIDE
+    cell = lax.broadcasted_iota(jnp.int32, (PIECES, CELLS), 1)
+    for e in range(2 * ROWS):
+        wanted = jnp.broadcast_to(maps_ref[:, e : e + 1], (PIECES, CELLS))
+        same = jnp.where(cell == wanted, 1.0, 0.0).astype(jnp.bfloat16)
+        hot[e * PIECES : (e + 1) * PIECES, :] = same
     found = lax.dot_general(
-        hot[...], held, (((1,), (1,)), ((), ())), preferred_element_type=jnp.float32
+        hot[...], held_ref[...], (((1,), (1,)), ((), ())), preferred_element_type=jnp.float32
     )
     for e in range(2 * ROWS):
-        for t in range(many // COLS):
+        for t in range(HELD // COLS):
             part = found[e * PIECES : (e + 1) * PIECES, t * COLS : (t + 1) * COLS]
             turned[t, pl.ds(e, PIECES, stride=2 * ROWS), :] = part
 
@@ -141,7 +164,7 @@
         for u in range(8):
             g = i * 8 + u
             at = pl.multiple_of(g * 2 * ROWS, 8)
-            for t in range(many // COLS):
+            for t in range(HELD // COLS):
                 lanes = min(COLS, bins - t * COLS)
                 value = turned[t, pl.ds(at, 2 * ROWS), :lanes].astype(jnp.bfloat16)
                 out_ref[g, :, t * COLS : t * COLS + lanes] = value
@@ -150,23 +173,19 @@
     lax.fori_loop(0, PIECES // 8, narrower, 0)
 
 
-def pick(*operands):
+def pick(maps, held):
     vmem = pl.BlockSpec(memory_space=pltpu.VMEM)
-    part = FLAT // SIDE
     return pl.pallas_call(
         pick_kernel,
-        out_shape=jax.ShapeDtypeStruct((PIECES, 2 * ROWS, part // ROWS), jnp.bfloat16),
-        in_specs=[vmem, pl.BlockSpec(memory_space=pl.ANY)] + [vmem] * 3,
+        out_shape=jax.ShapeDtypeStruct((PIECES, 2 * ROWS, BINS // SIDE), jnp.bfloat16),
+        in_specs=[vmem] * 2,
         out_specs=vmem,
         scratch_shapes=[
-            pltpu.VMEM((3 * COLS * ROWS, COLS), jnp.float32),
-            pltpu.VMEM((3, PIECES * 2 * ROWS, COLS), jnp.float32),
+            pltpu.VMEM((HELD // COLS, PIECES * 2 * ROWS, COLS), jnp.float32),
             pltpu.VMEM((PIECES * 2 * ROWS, CELLS), jnp.bfloat16),
-            pltpu.VMEM((part, COLS), jnp.bfloat16),
-            pltpu.SemaphoreType.DMA,
         ],
         compiler_params=pltpu.CompilerParams(vmem_limit_bytes=SMALL_BYTES),
-    )(*operands)
+    )(maps, held)
 
 
 def prepare_kernel(spec_ref, depth_ref, wet_ref, frac_ref, near_ref, stat_ref, dens):
@@ -678,7 +697,7 @@
     near, near_statics = prepare(spec, depth_factor, wet_mask, frac_index)
     near = swap(near)
     near_statics = swap(near_statics)
-    picked = lax.all_to_all(pick(maps, spec, *held), "grid", 0, 0)
+    picked = lax.all_to_all(pick(maps, join_held(spec, *held)), "grid", 0, 0)
     picked = jnp.concatenate([picked[hub] for hub in hubs], axis=1)
     far = swap(picked)
 

time: 108 us -> 108 us (level)
  blocking collectives: 49.7 us -> 35.5 us
  starting transfers between devices: 25.8 us -> 35.4 us
  waiting for transfers between devices: 14 us -> 18.1 us
    all_to_all x1 -> x0, blocking collectives: 14.2 us -> none  [on_device(): maps = lax.all_to_all(maps, 'grid', 0, 0)]
    all_to_all x1 -> x2, starting transfers between devices: 10.1 us -> 19.7 us  [the longest x1 10.1 us: on_device(): picked = lax.all_to_all(pick(maps, join_held(spec, *held)), 'grid', 0, 0)]
    all_to_all x1 -> x2, waiting for transfers between devices: 4.68 us -> 8.74 us  [the longest x1 4.68 us: on_device(): picked = lax.all_to_all(pick(maps, join_held(spec, *held)), 'grid', 0, 0)]
  transfers between devices with their start and end apart: 15 -> 16, of which waited for: 5 -> 6; matrix products, arithmetic and copies ran while one was open for 0% -> 0% of each run, Pallas kernels for 1% -> 1%
where the time goes in v1:
time: 108 us; the launch traced here: 107 us
  blocking collectives  35.5 us (33%)
  starting transfers between devices  35.4 us (33%)
  waiting for transfers between devices  18.1 us (17%)
  Pallas kernels  17.6 us (16%)
    all_to_all x1, blocking collectives, on_device(): copies = average(lax.all_to_all(pieces, 'grid', 0, 0))  27.1 us
    pallas_call x1, Pallas kernels, evolve(): pl.pallas_call(step_kernel, out_shape=(jax.ShapeDtypeStruct((FLAT, COLS),...  10.7 us
    all_to_all x1, starting transfers between devices, on_device(): picked = lax.all_to_all(pick(maps, join_held(spec, *held)), 'grid', 0, 0)  10.1 us
    all_to_all x1, starting transfers between devices, on_device(): maps = lax.all_to_all(maps, 'grid', 0, 0)  9.61 us
    all_to_all x1, blocking collectives, on_device(): gathered = lax.all_to_all(copies, 'grid', 0, 0, axis_index_groups=cubes)  8.39 us
    ppermute x4, waiting for transfers between devices, on_device(): lax.ppermute(relayed, 'grid', [(device, parent)])  6.08 us
    ppermute x3, starting transfers between devices, on_device(): lax.ppermute(part, 'grid', [(parent, hub)])  5.36 us
    ppermute x4, starting transfers between devices, on_device(): lax.ppermute(relayed, 'grid', [(device, parent)])  5.16 us
  transfers between devices with their start and end apart: 16, of which 6 were waited for; matrix products, arithmetic and copies ran while one was open for 0% of the time, Pallas kernels for 1%

profile of v1, /device:TPU:126, one launch (start us, length us, event | category | flops | bytes accessed | tf_op | source)
XLA Modules:
  0.0 107.1 jit_solution(3224525094257345861)
XLA Ops:
  0.0 2.4 %shard_map.146 = (s32[64,128]{1,0:T(8,128)}, bf16[1296,128]{1,0:T(8,128)(2,1)}, bf16[1296,128]{1,0:T(8,128)(2,1)}, bf16[1296,128]{1,0:T(8,128)(2,1)}) custom-call(s32[2,4]{1,0:T(2,128)} %bitcast.21, bf16[5184,128]{1,0:T(8,128)(2,1)} %bitcast.15), custom_call_target="tpu_custom_call" | custom-call | tf_op jit(solution)/shard_map/pallas_call | solution.py:96
  2.4 2.7 %collective-permute-start.1 = (bf16[1296,128]{1,0:T(8,128)(2,1)}, bf16[1296,128]{1,0:T(8,128)(2,1)S(1)}, u32[]{:S(2)}, u32[]{:S(2)}) collective-permute-start(bf16[1296,128]{1,0:T(8,128)(2,1)} %get-tuple-element.15), channel_id=1, source_target_pairs={{126,124},{127,125}} | collective-permute-start | bytes 995336 | tf_op jit(solution)/shard_map/ppermute | solution.py:695
  5.2 1.3 %collective-permute-start.2 = (bf16[1296,128]{1,0:T(8,128)(2,1)}, bf16[1296,128]{1,0:T(8,128)(2,1)S(1)}, u32[]{:S(2)}, u32[]{:S(2)}) collective-permute-start(bf16[1296,128]{1,0:T(8,128)(2,1)} %get-tuple-element.16), channel_id=1, source_target_pairs={{126,118},{127,119}} | collective-permute-start | bytes 995336 | tf_op jit(solution)/shard_map/ppermute | solution.py:695
  6.5 1.3 %collective-permute-start.3 = (bf16[1296,128]{1,0:T(8,128)(2,1)}, bf16[1296,128]{1,0:T(8,128)(2,1)S(1)}, u32[]{:S(2)}, u32[]{:S(2)}) collective-permute-start(bf16[1296,128]{1,0:T(8,128)(2,1)} %get-tuple-element.17), channel_id=1, source_target_pairs={{126,94},{127,95}} | collective-permute-start | bytes 995336 | tf_op jit(solution)/shard_map/ppermute | solution.py:695
  7.8 9.6 %all-to-all-start = ((s32[64,1,128]{2,1,0:T(1,128)}), s32[64,1,128]{2,1,0:T(1,128)S(1)}, u32[]{:S(2)}, u32[]{:S(2)}) async-start(s32[64,1,128]{2,1,0:T(1,128)} %bitcast.20), calls=%async_computation | async-start | bytes 65536 | tf_op jit(solution)/shard_map/all_to_all | solution.py:696
  17.4 0.0 collective-permute-done.1.a_ref
  17.4 0.0 collective-permute-done.2.b_ref
  17.5 0.0 collective-permute-done.3.c_ref
  17.5 0.4 shard_map.147.held_ref
  17.9 0.0 copy-start.1
  17.9 0.0 copy-start.2
  17.9 0.0 copy-start.3
  18.0 4.1 %all-to-all-done = s32[64,1,128]{2,1,0:T(1,128)S(1)} async-done(((s32[64,1,128]{2,1,0:T(1,128)}), s32[64,1,128]{2,1,0:T(1,128)S(1)}, u32[]{:S(2)}, u32[]{:S(2)}) %all-to-all-start) | async-done | bytes 32800 | tf_op jit(solution)/shard_map/all_to_all | solution.py:696
  22.0 1.4 %shard_map.148 = bf16[64,8,324]{2,1,0:T(8,128)(2,1)} custom-call(s32[64,128]{1,0:T(8,128)S(1)} %bitcast.19, bf16[384,512]{1,0:T(8,128)(2,1)S(1)} %shard_map.147.held_ref), custom_call_target="tpu_custom_call" | custom-call | tf_op jit(solution)/shard_map/pallas_call | solution.py:178
  23.4 0.0 copy-start.8
  23.4 0.0 copy-start.9
  23.4 0.0 copy-start.10
  23.5 0.0 copy-start.11
  23.5 10.1 %all-to-all-start.1 = ((bf16[64,8,324]{2,1,0:T(8,128)(2,1)}), bf16[64,8,324]{2,1,0:T(8,128)(2,1)S(1)}, u32[]{:S(2)}, u32[]{:S(2)}) async-start(bf16[64,8,324]{2,1,0:T(8,128)(2,1)} %shard_map.148), calls=%async_computation.1 | async-start | bytes 786432 | tf_op jit(solution)/shard_map/all_to_all | solution.py:700
  33.6 0.7 shard_map.145
  34.3 0.1 collective-permute-start
  34.4 0.5 collective-permute-start.5
  34.8 4.7 %all-to-all-done.1 = bf16[64,8,324]{2,1,0:T(8,128)(2,1)S(1)} async-done(((bf16[64,8,324]{2,1,0:T(8,128)(2,1)}), bf16[64,8,324]{2,1,0:T(8,128)(2,1)S(1)}, u32[]{:S(2)}, u32[]{:S(2)}) %all-to-all-start.1) | async-done | bytes 331808 | tf_op jit(solution)/shard_map/all_to_all | solution.py:700
  39.5 0.1 concatenate.3.edge_ref
  39.6 0.1 collective-permute-start.4
  39.8 0.0 collective-permute-done.5.stat_ref
  39.8 1.1 %collective-permute-done.4.far_ref = bf16[8,1296]{1,0:T(8,128)(2,1)S(1)} collective-permute-done((bf16[8,1296]{1,0:T(8,128)(2,1)S(1)}, bf16[8,1296]{1,0:T(8,128)(2,1)S(1)}, u32[]{:S(2)}, u32[]{:S(2)}) %collective-permute-start.4) | collective-permute-done | bytes 20768 | tf_op jit(solution)/shard_map/ppermute | solution.py:676
  41.0 10.7 %shard_map.149 = (bf16[5184,128]{1,0:T(8,128)(2,1)}, s16[64,88,128]{2,1,0:T(8,128)(2,1)S(1)}) custom-call(s32[1296]{0:T(1024)S(1)} %get-tuple-element.26.plus_ref, s32[1296]{0:T(1024)S(1)} %get-tuple-element.25.minus_ref, f32[36]{0:T(128)S(1)} %copy-done.11, f32[36]{0:T(128)S(1)} %copy-done.5, bf16[5184,128]{1,0:T(8,128)(2,1)S(1)} %bitcast.18, ...), custom_call_target="tpu_custom_call" | custom-call | flops 1400000000 | bytes 10000000 | tf_op jit(solution)/shard_map/pallas_call | solution.py:524
  51.7 27.1 %all_to_all.26.pieces_ref = s16[64,88,128]{2,1,0:T(8,128)(2,1)S(1)} all-to-all(s16[64,88,128]{2,1,0:T(8,128)(2,1)S(1)} %get-tuple-element.19), channel_id=1, replica_groups=mesh['grid'=64,'cell'=2] {'grid'}, dimensions={0} | all-to-all | bytes 2883584 | tf_op jit(solution)/shard_map/all_to_all | solution.py:725
  78.8 0.5 shard_map.150
  79.3 8.4 %all_to_all.27.refs_0_ = bf16[8,88,128]{2,1,0:T(8,128)(2,1)S(1)} all-to-all(bf16[8,88,128]{2,1,0:T(8,128)(2,1)S(1)} %shard_map.150), channel_id=1, replica_groups={{0,2,8,10,32,34,40,42},{4,6,12,14,36,38,44,46},{16,18,24,26,48,50,56,58..., dimensions={0} | all-to-all | bytes 360448 | tf_op jit(solution)/shard_map/all_to_all | solution.py:728
  87.7 0.7 collective-permute-start.9
  88.4 1.3 %collective-permute-start.8 = (bf16[8,88,128]{2,1,0:T(8,128)(2,1)S(1)}, bf16[8,88,128]{2,1,0:T(8,128)(2,1)S(1)}, u32[]{:S(2)}, u32[]{:S(2)}) collective-permute-start(bf16[8,88,128]{2,1,0:T(8,128)(2,1)S(1)} %all_to_all.27.refs_0_), channel_id=1, source_target_pairs={{30,126},{31,127}} | collective-permute-start | bytes 540680 | tf_op jit(solution)/shard_map/ppermute | solution.py:734
  89.7 1.3 %collective-permute-start.7 = (bf16[8,88,128]{2,1,0:T(8,128)(2,1)S(1)}, bf16[8,88,128]{2,1,0:T(8,128)(2,1)S(1)}, u32[]{:S(2)}, u32[]{:S(2)}) collective-permute-start(bf16[8,88,128]{2,1,0:T(8,128)(2,1)S(1)} %all_to_all.27.refs_0_), channel_id=1, source_target_pairs={{102,126},{103,127}} | collective-permute-start | bytes 540680 | tf_op jit(solution)/shard_map/ppermute | solution.py:734
  91.0 1.3 %collective-permute-start.6 = (bf16[8,88,128]{2,1,0:T(8,128)(2,1)S(1)}, bf16[8,88,128]{2,1,0:T(8,128)(2,1)S(1)}, u32[]{:S(2)}, u32[]{:S(2)}) collective-permute-start(bf16[8,88,128]{2,1,0:T(8,128)(2,1)S(1)} %all_to_all.27.refs_0_), channel_id=1, source_target_pairs={{120,126},{121,127}} | collective-permute-start | bytes 540680 | tf_op jit(solution)/shard_map/ppermute | solution.py:734
  92.3 0.0 collective-permute-done.9
  92.3 1.3 %collective-permute-start.13 = (bf16[8,88,128]{2,1,0:T(8,128)(2,1)S(1)}, bf16[8,88,128]{2,1,0:T(8,128)(2,1)S(1)}, u32[]{:S(2)}, u32[]{:S(2)}) collective-permute-start(bf16[8,88,128]{2,1,0:T(8,128)(2,1)S(1)} %collective-permute-done.9), channel_id=1, source_target_pairs={{30,126},{31,127}} | collective-permute-start | bytes 540680 | tf_op jit(solution)/shard_map/ppermute | solution.py:735
  93.6 1.3 %collective-permute-start.12 = (bf16[8,88,128]{2,1,0:T(8,128)(2,1)S(1)}, bf16[8,88,128]{2,1,0:T(8,128)(2,1)S(1)}, u32[]{:S(2)}, u32[]{:S(2)}) collective-permute-start(bf16[8,88,128]{2,1,0:T(8,128)(2,1)S(1)} %collective-permute-done.9), channel_id=1, source_target_pairs={{94,126},{95,127}} | collective-permute-start | bytes 540680 | tf_op jit(solution)/shard_map/ppermute | solution.py:735
  94.9 2.1 %collective-permute-done.8.refs_3_ = bf16[8,88,128]{2,1,0:T(8,128)(2,1)S(1)} collective-permute-done((bf16[8,88,128]{2,1,0:T(8,128)(2,1)S(1)}, bf16[8,88,128]{2,1,0:T(8,128)(2,1)S(1)}, u32[]{:S(2)}, u32[]{:S(2)}) %collective-permute-start.8) | collective-permute-done | bytes 180256 | tf_op jit(solution)/shard_map/ppermute | solution.py:734
  97.0 1.3 %collective-permute-start.11 = (bf16[8,88,128]{2,1,0:T(8,128)(2,1)S(1)}, bf16[8,88,128]{2,1,0:T(8,128)(2,1)S(1)}, u32[]{:S(2)}, u32[]{:S(2)}) collective-permute-start(bf16[8,88,128]{2,1,0:T(8,128)(2,1)S(1)} %collective-permute-done.9), channel_id=1, source_target_pairs={{118,126},{119,127}} | collective-permute-start | bytes 540680 | tf_op jit(solution)/shard_map/ppermute | solution.py:735
  98.3 0.0 collective-permute-done.7.refs_2_
  98.3 1.3 %collective-permute-start.10 = (bf16[8,88,128]{2,1,0:T(8,128)(2,1)S(1)}, bf16[8,88,128]{2,1,0:T(8,128)(2,1)S(1)}, u32[]{:S(2)}, u32[]{:S(2)}) collective-permute-start(bf16[8,88,128]{2,1,0:T(8,128)(2,1)S(1)} %collective-permute-done.9), channel_id=1, source_target_pairs={{124,126},{125,127}} | collective-permute-start | bytes 540680 | tf_op jit(solution)/shard_map/ppermute | solution.py:735
  99.6 0.0 collective-permute-done.6.refs_1_
  99.6 5.8 %collective-permute-done.13.refs_7_ = bf16[8,88,128]{2,1,0:T(8,128)(2,1)S(1)} collective-permute-done((bf16[8,88,128]{2,1,0:T(8,128)(2,1)S(1)}, bf16[8,88,128]{2,1,0:T(8,128)(2,1)S(1)}, u32[]{:S(2)}, u32[]{:S(2)}) %collective-permute-start.13) | collective-permute-done | bytes 180256 | tf_op jit(solution)/shard_map/ppermute | solution.py:735
  105.4 0.0 collective-permute-done.12.refs_6_
  105.4 0.0 collective-permute-done.11.refs_5_
  105.4 0.3 collective-permute-done.10.refs_4_
  105.7 1.4 %shard_map.151 = bf16[5184,128]{1,0:T(8,128)(2,1)} custom-call(bf16[8,88,128]{2,1,0:T(8,128)(2,1)S(1)} %all_to_all.27.refs_0_, bf16[8,88,128]{2,1,0:T(8,128)(2,1)S(1)} %collective-permute-done.6.refs_1_, bf16[8,88,128]{2,1,0:T(8,128)(2,1)S(1)} %collective-permute-done.7.refs_2_, ...), custom_call_target="tpu_custom_call", output_to_operand_aliasing={{}: (8, {})} | custom-call | tf_op jit(solution)/shard_map/pallas_call | solution.py:634
  (24 shorter events, 0.1 us)
Async XLA Ops:
  0.0 17.5 %copy-start = (bf16[1296,4,128]{2,1,0:T(4,128)(2,1)S(1)}, bf16[1296,4,128]{2,1,0:T(4,128)(2,1)}, u32[]{:S(2)}) copy-start(bf16[1296,4,128]{2,1,0:T(4,128)(2,1)} %param.15) | copy-start | bytes 3981316
  2.4 15.0 %collective-permute-start.1 = (bf16[1296,128]{1,0:T(8,128)(2,1)}, bf16[1296,128]{1,0:T(8,128)(2,1)S(1)}, u32[]{:S(2)}, u32[]{:S(2)}) collective-permute-start(bf16[1296,128]{1,0:T(8,128)(2,1)} %get-tuple-element.15), channel_id=1, source_target_pairs={{126,124},{127,125}} | collective-permute-start | bytes 995336 | tf_op jit(solution)/shard_map/ppermute | solution.py:695
  5.2 12.3 %collective-permute-start.2 = (bf16[1296,128]{1,0:T(8,128)(2,1)}, bf16[1296,128]{1,0:T(8,128)(2,1)S(1)}, u32[]{:S(2)}, u32[]{:S(2)}) collective-permute-start(bf16[1296,128]{1,0:T(8,128)(2,1)} %get-tuple-element.16), channel_id=1, source_target_pairs={{126,118},{127,119}} | collective-permute-start | bytes 995336 | tf_op jit(solution)/shard_map/ppermute | solution.py:695
  6.5 11.0 %collective-permute-start.3 = (bf16[1296,128]{1,0:T(8,128)(2,1)}, bf16[1296,128]{1,0:T(8,128)(2,1)S(1)}, u32[]{:S(2)}, u32[]{:S(2)}) collective-permute-start(bf16[1296,128]{1,0:T(8,128)(2,1)} %get-tuple-element.17), channel_id=1, source_target_pairs={{126,94},{127,95}} | collective-permute-start | bytes 995336 | tf_op jit(solution)/shard_map/ppermute | solution.py:695
  7.8 14.2 %all-to-all-start = ((s32[64,1,128]{2,1,0:T(1,128)}), s32[64,1,128]{2,1,0:T(1,128)S(1)}, u32[]{:S(2)}, u32[]{:S(2)}) async-start(s32[64,1,128]{2,1,0:T(1,128)} %bitcast.20), calls=%async_computation | async-start | bytes 65536 | tf_op jit(solution)/shard_map/all_to_all | solution.py:696
  17.9 15.6 %copy-start.1 = (f32[4,128]{1,0:T(4,128)S(1)}, f32[4,128]{1,0:T(4,128)}, u32[]{:S(2)}) copy-start(f32[4,128]{1,0:T(4,128)} %depth_ref.3) | copy-start | bytes 6148
  17.9 15.6 %copy-start.2 = (s32[4,128]{1,0:T(4,128)S(1)}, s32[4,128]{1,0:T(4,128)}, u32[]{:S(2)}) copy-start(s32[4,128]{1,0:T(4,128)} %wet_ref.3) | copy-start | bytes 6148
  17.9 15.6 %copy-start.3 = (s32[4,128]{1,0:T(4,128)S(1)}, s32[4,128]{1,0:T(4,128)}, u32[]{:S(2)}) copy-start(s32[4,128]{1,0:T(4,128)} %frac_ref.3) | copy-start | bytes 6148
  22.0 17.7 %copy-start.12 = (s32[1296]{0:T(1024)S(1)}, s32[1296]{0:T(1024)}, u32[]{:S(2)}) copy-start(s32[1296]{0:T(1024)} %param.22) | copy-start | bytes 15556
  22.0 17.7 %copy-start.13 = (s32[1296]{0:T(1024)S(1)}, s32[1296]{0:T(1024)}, u32[]{:S(2)}) copy-start(s32[1296]{0:T(1024)} %param.21) | copy-start | bytes 15556
  23.4 17.5 %copy-start.4 = (s32[4,128]{1,0:T(4,128)S(1)}, s32[4,128]{1,0:T(4,128)}, u32[]{:S(2)}) copy-start(s32[4,128]{1,0:T(4,128)} %target_ref.1) | copy-start | bytes 6148
  23.4 17.5 %copy-start.5 = (f32[36]{0:T(128)S(1)}, f32[36]{0:T(128)}, u32[]{:S(2)}) copy-start(f32[36]{0:T(128)} %coef_ref.1) | copy-start | bytes 436
  23.4 17.5 %copy-start.6 = (f32[144,128]{1,0:T(8,128)S(1)}, f32[144,128]{1,0:T(8,128)}, u32[]{:S(2)}) copy-start(f32[144,128]{1,0:T(8,128)} %constant.19.clone.sin_ref) | copy-start | bytes 221188
  23.4 17.5 %copy-start.7 = (f32[144,128]{1,0:T(8,128)S(1)}, f32[144,128]{1,0:T(8,128)}, u32[]{:S(2)}) copy-start(f32[144,128]{1,0:T(8,128)} %constant.18.clone.cos_ref) | copy-start | bytes 221188
  23.4 17.5 %copy-start.8 = (bf16[2,16,768]{2,1,0:T(8,128)(2,1)S(1)}, bf16[2,16,768]{2,1,0:T(8,128)(2,1)}, u32[]{:S(2)}) copy-start(bf16[2,16,768]{2,1,0:T(8,128)(2,1)} %constant.17.clone.spot_ref) | copy-start | bytes 147460
  23.4 17.5 %copy-start.9 = (f32[72,128]{1,0:T(8,128)S(1)}, f32[72,128]{1,0:T(8,128)}, u32[]{:S(2)}) copy-start(f32[72,128]{1,0:T(8,128)} %constant.21.clone.sinb_ref) | copy-start | bytes 110596
  23.4 17.5 %copy-start.10 = (f32[72,128]{1,0:T(8,128)S(1)}, f32[72,128]{1,0:T(8,128)}, u32[]{:S(2)}) copy-start(f32[72,128]{1,0:T(8,128)} %constant.20.clone.cosb_ref) | copy-start | bytes 110596
  23.5 17.5 %copy-start.11 = (f32[36]{0:T(128)S(1)}, f32[36]{0:T(128)}, u32[]{:S(2)}) copy-start(f32[36]{0:T(128)} %constant.16.clone.speed_ref) | copy-start | bytes 436
  23.5 16.1 %all-to-all-start.1 = ((bf16[64,8,324]{2,1,0:T(8,128)(2,1)}), bf16[64,8,324]{2,1,0:T(8,128)(2,1)S(1)}, u32[]{:S(2)}, u32[]{:S(2)}) async-start(bf16[64,8,324]{2,1,0:T(8,128)(2,1)} %shard_map.148), calls=%async_computation.1 | async-start | bytes 786432 | tf_op jit(solution)/shard_map/all_to_all | solution.py:700
  34.3 5.5 %collective-permute-start = (bf16[2,1296,128]{2,1,0:T(8,128)(2,1)S(1)}, bf16[2,1296,128]{2,1,0:T(8,128)(2,1)S(1)}, u32[]{:S(2)}, u32[]{:S(2)}) collective-permute-start(bf16[2,1296,128]{2,1,0:T(8,128)(2,1)S(1)} %get-tuple-element.13), channel_id=1, source_target_pairs={{0,1},{1,0},{2,3},{3,2},{4,5},{5,4},{6,7},{7,6},{8,9},{9,8},{10,11... | collective-permute-start | bytes 1990664 | tf_op jit(solution)/shard_map/ppermute | solution.py:676
  34.4 5.4 %collective-permute-start.5 = (f32[8,128]{1,0:T(8,128)S(1)}, f32[8,128]{1,0:T(8,128)S(1)}, u32[]{:S(2)}, u32[]{:S(2)}) collective-permute-start(f32[8,128]{1,0:T(8,128)S(1)} %get-tuple-element.18), channel_id=1, source_target_pairs={{0,1},{1,0},{2,3},{3,2},{4,5},{5,4},{6,7},{7,6},{8,9},{9,8},{10,11... | collective-permute-start | bytes 12296 | tf_op jit(solution)/shard_map/ppermute | solution.py:676
  39.6 1.3 %collective-permute-start.4 = (bf16[8,1296]{1,0:T(8,128)(2,1)S(1)}, bf16[8,1296]{1,0:T(8,128)(2,1)S(1)}, u32[]{:S(2)}, u32[]{:S(2)}) collective-permute-start(bf16[8,1296]{1,0:T(8,128)(2,1)S(1)} %concatenate.3.edge_ref), channel_id=1, source_target_pairs={{0,1},{1,0},{2,3},{3,2},{4,5},{5,4},{6,7},{7,6},{8,9},{9,8},{10,11... | collective-permute-start | bytes 62216 | tf_op jit(solution)/shard_map/ppermute | solution.py:676
  87.7 4.6 %collective-permute-start.9 = (bf16[8,88,128]{2,1,0:T(8,128)(2,1)S(1)}, bf16[8,88,128]{2,1,0:T(8,128)(2,1)S(1)}, u32[]{:S(2)}, u32[]{:S(2)}) collective-permute-start(bf16[8,88,128]{2,1,0:T(8,128)(2,1)S(1)} %all_to_all.27.refs_0_), channel_id=1, source_target_pairs={{98,124},{14,118},{56,94},{0,30},{99,125},{15,119},{57,95},{1,31}} | collective-permute-start | bytes 540680 | tf_op jit(solution)/shard_map/ppermute | solution.py:733
  88.4 8.6 %collective-permute-start.8 = (bf16[8,88,128]{2,1,0:T(8,128)(2,1)S(1)}, bf16[8,88,128]{2,1,0:T(8,128)(2,1)S(1)}, u32[]{:S(2)}, u32[]{:S(2)}) collective-permute-start(bf16[8,88,128]{2,1,0:T(8,128)(2,1)S(1)} %all_to_all.27.refs_0_), channel_id=1, source_target_pairs={{30,126},{31,127}} | collective-permute-start | bytes 540680 | tf_op jit(solution)/shard_map/ppermute | solution.py:734
  89.7 8.6 %collective-permute-start.7 = (bf16[8,88,128]{2,1,0:T(8,128)(2,1)S(1)}, bf16[8,88,128]{2,1,0:T(8,128)(2,1)S(1)}, u32[]{:S(2)}, u32[]{:S(2)}) collective-permute-start(bf16[8,88,128]{2,1,0:T(8,128)(2,1)S(1)} %all_to_all.27.refs_0_), channel_id=1, source_target_pairs={{102,126},{103,127}} | collective-permute-start | bytes 540680 | tf_op jit(solution)/shard_map/ppermute | solution.py:734
  91.0 8.6 %collective-permute-start.6 = (bf16[8,88,128]{2,1,0:T(8,128)(2,1)S(1)}, bf16[8,88,128]{2,1,0:T(8,128)(2,1)S(1)}, u32[]{:S(2)}, u32[]{:S(2)}) collective-permute-start(bf16[8,88,128]{2,1,0:T(8,128)(2,1)S(1)} %all_to_all.27.refs_0_), channel_id=1, source_target_pairs={{120,126},{121,127}} | collective-permute-start | bytes 540680 | tf_op jit(solution)/shard_map/ppermute | solution.py:734
  92.3 13.1 %collective-permute-start.13 = (bf16[8,88,128]{2,1,0:T(8,128)(2,1)S(1)}, bf16[8,88,128]{2,1,0:T(8,128)(2,1)S(1)}, u32[]{:S(2)}, u32[]{:S(2)}) collective-permute-start(bf16[8,88,128]{2,1,0:T(8,128)(2,1)S(1)} %collective-permute-done.9), channel_id=1, source_target_pairs={{30,126},{31,127}} | collective-permute-start | bytes 540680 | tf_op jit(solution)/shard_map/ppermute | solution.py:735
  93.6 11.8 %collective-permute-start.12 = (bf16[8,88,128]{2,1,0:T(8,128)(2,1)S(1)}, bf16[8,88,128]{2,1,0:T(8,128)(2,1)S(1)}, u32[]{:S(2)}, u32[]{:S(2)}) collective-permute-start(bf16[8,88,128]{2,1,0:T(8,128)(2,1)S(1)} %collective-permute-done.9), channel_id=1, source_target_pairs={{94,126},{95,127}} | collective-permute-start | bytes 540680 | tf_op jit(solution)/shard_map/ppermute | solution.py:735
  97.0 8.4 %collective-permute-start.11 = (bf16[8,88,128]{2,1,0:T(8,128)(2,1)S(1)}, bf16[8,88,128]{2,1,0:T(8,128)(2,1)S(1)}, u32[]{:S(2)}, u32[]{:S(2)}) collective-permute-start(bf16[8,88,128]{2,1,0:T(8,128)(2,1)S(1)} %collective-permute-done.9), channel_id=1, source_target_pairs={{118,126},{119,127}} | collective-permute-start | bytes 540680 | tf_op jit(solution)/shard_map/ppermute | solution.py:735
  98.3 7.4 %collective-permute-start.10 = (bf16[8,88,128]{2,1,0:T(8,128)(2,1)S(1)}, bf16[8,88,128]{2,1,0:T(8,128)(2,1)S(1)}, u32[]{:S(2)}, u32[]{:S(2)}) collective-permute-start(bf16[8,88,128]{2,1,0:T(8,128)(2,1)S(1)} %collective-permute-done.9), channel_id=1, source_target_pairs={{124,126},{125,127}} | collective-permute-start | bytes 540680 | tf_op jit(solution)/shard_map/ppermute | solution.py:735

commit v2 on v1

--- a/solution.py
+++ b/solution.py
@@ -19,7 +19,7 @@
 FLAT = BINS * ROWS
 PAD = 8
 PIECES = SIDE**3
-TOGETHER = 6
+TOGETHER = 9
 PIECE = FLAT // PIECES
 TALL = 88
 BLOCK = 72
@@ -560,8 +560,8 @@
 
     def add(i, carry):
         sums, weights, number = carry
-        for u in range(4):
-            piece = pieces_ref[4 * i + u].astype(jnp.int32).astype(jnp.float32)
+        for u in range(8):
+            piece = pieces_ref[8 * i + u].astype(jnp.int32).astype(jnp.float32)
             rest = piece[TALL - 8 :]
             at = PIECE % 8
             turned = [pltpu.roll(rest, shift - at, 0) for shift in (8, ROWS)]
@@ -573,7 +573,7 @@
 
     zero = jnp.zeros((8, COLS), jnp.float32)
     carry = ((zero,) * blocks, zero, zero)
-    sums, weights, number = lax.fori_loop(0, PIECES // 4, add, carry)
+    sums, weights, number = lax.fori_loop(0, PIECES // 8, add, carry)
     scale = 1.0 / (UNIT * STEPS * number)
     mean = jnp.concatenate([(part + OFFSET * weights) * scale for part in sums], axis=0)
     mean = mean.astype(jnp.bfloat16)

time: 108 us -> 108 us (level)
  no operation moved by 1% of the time
where the time goes in v2:
time: 108 us; the launch traced here: 107 us
  blocking collectives  35.5 us (33%)
  starting transfers between devices  35.4 us (33%)
  waiting for transfers between devices  18.1 us (17%)
  Pallas kernels  17.5 us (16%)
    all_to_all x1, blocking collectives, on_device(): copies = average(lax.all_to_all(pieces, 'grid', 0, 0))  27.1 us
    pallas_call x1, Pallas kernels, evolve(): pl.pallas_call(step_kernel, out_shape=(jax.ShapeDtypeStruct((FLAT, COLS),...  10.6 us
    all_to_all x1, starting transfers between devices, on_device(): picked = lax.all_to_all(pick(maps, join_held(spec, *held)), 'grid', 0, 0)  10.1 us
    all_to_all x1, starting transfers between devices, on_device(): maps = lax.all_to_all(maps, 'grid', 0, 0)  9.61 us
    all_to_all x1, blocking collectives, on_device(): gathered = lax.all_to_all(copies, 'grid', 0, 0, axis_index_groups=cubes)  8.39 us
    ppermute x4, waiting for transfers between devices, on_device(): lax.ppermute(relayed, 'grid', [(device, parent)])  6.08 us
    ppermute x3, starting transfers between devices, on_device(): lax.ppermute(part, 'grid', [(parent, hub)])  5.36 us
    ppermute x4, starting transfers between devices, on_device(): lax.ppermute(relayed, 'grid', [(device, parent)])  5.16 us
  transfers between devices with their start and end apart: 16, of which 6 were waited for; matrix products, arithmetic and copies ran while one was open for 0% of the time, Pallas kernels for 1%

profile of v2, /device:TPU:126, one launch (start us, length us, event | category | flops | bytes accessed | tf_op | source)
XLA Modules:
  0.0 107.0 jit_solution(18110945852409789789)
XLA Ops:
  0.0 2.4 %shard_map.146 = (s32[64,128]{1,0:T(8,128)}, bf16[1296,128]{1,0:T(8,128)(2,1)}, bf16[1296,128]{1,0:T(8,128)(2,1)}, bf16[1296,128]{1,0:T(8,128)(2,1)}) custom-call(s32[2,4]{1,0:T(2,128)} %bitcast.21, bf16[5184,128]{1,0:T(8,128)(2,1)} %bitcast.15), custom_call_target="tpu_custom_call" | custom-call | tf_op jit(solution)/shard_map/pallas_call | solution.py:96
  2.4 2.7 %collective-permute-start.1 = (bf16[1296,128]{1,0:T(8,128)(2,1)}, bf16[1296,128]{1,0:T(8,128)(2,1)S(1)}, u32[]{:S(2)}, u32[]{:S(2)}) collective-permute-start(bf16[1296,128]{1,0:T(8,128)(2,1)} %get-tuple-element.15), channel_id=1, source_target_pairs={{126,124},{127,125}} | collective-permute-start | bytes 995336 | tf_op jit(solution)/shard_map/ppermute | solution.py:695
  5.2 1.3 %collective-permute-start.2 = (bf16[1296,128]{1,0:T(8,128)(2,1)}, bf16[1296,128]{1,0:T(8,128)(2,1)S(1)}, u32[]{:S(2)}, u32[]{:S(2)}) collective-permute-start(bf16[1296,128]{1,0:T(8,128)(2,1)} %get-tuple-element.16), channel_id=1, source_target_pairs={{126,118},{127,119}} | collective-permute-start | bytes 995336 | tf_op jit(solution)/shard_map/ppermute | solution.py:695
  6.5 1.3 %collective-permute-start.3 = (bf16[1296,128]{1,0:T(8,128)(2,1)}, bf16[1296,128]{1,0:T(8,128)(2,1)S(1)}, u32[]{:S(2)}, u32[]{:S(2)}) collective-permute-start(bf16[1296,128]{1,0:T(8,128)(2,1)} %get-tuple-element.17), channel_id=1, source_target_pairs={{126,94},{127,95}} | collective-permute-start | bytes 995336 | tf_op jit(solution)/shard_map/ppermute | solution.py:695
  7.8 9.6 %all-to-all-start = ((s32[64,1,128]{2,1,0:T(1,128)}), s32[64,1,128]{2,1,0:T(1,128)S(1)}, u32[]{:S(2)}, u32[]{:S(2)}) async-start(s32[64,1,128]{2,1,0:T(1,128)} %bitcast.20), calls=%async_computation | async-start | bytes 65536 | tf_op jit(solution)/shard_map/all_to_all | solution.py:696
  17.4 0.0 collective-permute-done.1.a_ref
  17.4 0.0 collective-permute-done.2.b_ref
  17.5 0.0 collective-permute-done.3.c_ref
  17.5 0.4 shard_map.147.held_ref
  17.9 0.0 copy-start.1
  17.9 0.0 copy-start.2
  17.9 0.0 copy-start.3
  18.0 4.1 %all-to-all-done = s32[64,1,128]{2,1,0:T(1,128)S(1)} async-done(((s32[64,1,128]{2,1,0:T(1,128)}), s32[64,1,128]{2,1,0:T(1,128)S(1)}, u32[]{:S(2)}, u32[]{:S(2)}) %all-to-all-start) | async-done | bytes 32800 | tf_op jit(solution)/shard_map/all_to_all | solution.py:696
  22.0 1.4 %shard_map.148 = bf16[64,8,324]{2,1,0:T(8,128)(2,1)} custom-call(s32[64,128]{1,0:T(8,128)S(1)} %bitcast.19, bf16[384,512]{1,0:T(8,128)(2,1)S(1)} %shard_map.147.held_ref), custom_call_target="tpu_custom_call" | custom-call | tf_op jit(solution)/shard_map/pallas_call | solution.py:178
  23.4 0.0 copy-start.8
  23.4 0.0 copy-start.9
  23.4 0.0 copy-start.10
  23.5 0.0 copy-start.11
  23.5 10.1 %all-to-all-start.1 = ((bf16[64,8,324]{2,1,0:T(8,128)(2,1)}), bf16[64,8,324]{2,1,0:T(8,128)(2,1)S(1)}, u32[]{:S(2)}, u32[]{:S(2)}) async-start(bf16[64,8,324]{2,1,0:T(8,128)(2,1)} %shard_map.148), calls=%async_computation.1 | async-start | bytes 786432 | tf_op jit(solution)/shard_map/all_to_all | solution.py:700
  33.6 0.7 shard_map.145
  34.3 0.1 collective-permute-start
  34.4 0.5 collective-permute-start.5
  34.8 4.7 %all-to-all-done.1 = bf16[64,8,324]{2,1,0:T(8,128)(2,1)S(1)} async-done(((bf16[64,8,324]{2,1,0:T(8,128)(2,1)}), bf16[64,8,324]{2,1,0:T(8,128)(2,1)S(1)}, u32[]{:S(2)}, u32[]{:S(2)}) %all-to-all-start.1) | async-done | bytes 331808 | tf_op jit(solution)/shard_map/all_to_all | solution.py:700
  39.5 0.1 concatenate.3.edge_ref
  39.6 0.1 collective-permute-start.4
  39.8 0.0 collective-permute-done.5.stat_ref
  39.8 0.0 collective-permute-done.near_ref
  39.8 1.1 %collective-permute-done.4.far_ref = bf16[8,1296]{1,0:T(8,128)(2,1)S(1)} collective-permute-done((bf16[8,1296]{1,0:T(8,128)(2,1)S(1)}, bf16[8,1296]{1,0:T(8,128)(2,1)S(1)}, u32[]{:S(2)}, u32[]{:S(2)}) %collective-permute-start.4) | collective-permute-done | bytes 20768 | tf_op jit(solution)/shard_map/ppermute | solution.py:676
  41.0 10.6 %shard_map.149 = (bf16[5184,128]{1,0:T(8,128)(2,1)}, s16[64,88,128]{2,1,0:T(8,128)(2,1)S(1)}) custom-call(s32[1296]{0:T(1024)S(1)} %get-tuple-element.26.plus_ref, s32[1296]{0:T(1024)S(1)} %get-tuple-element.25.minus_ref, f32[36]{0:T(128)S(1)} %copy-done.11, f32[36]{0:T(128)S(1)} %copy-done.5, bf16[5184,128]{1,0:T(8,128)(2,1)S(1)} %bitcast.18, ...), custom_call_target="tpu_custom_call" | custom-call | flops 1400000000 | bytes 10000000 | tf_op jit(solution)/shard_map/pallas_call | solution.py:524
  51.6 27.1 %all_to_all.26.pieces_ref = s16[64,88,128]{2,1,0:T(8,128)(2,1)S(1)} all-to-all(s16[64,88,128]{2,1,0:T(8,128)(2,1)S(1)} %get-tuple-element.19), channel_id=1, replica_groups=mesh['grid'=64,'cell'=2] {'grid'}, dimensions={0} | all-to-all | bytes 2883584 | tf_op jit(solution)/shard_map/all_to_all | solution.py:725
  78.7 0.5 shard_map.150
  79.2 8.4 %all_to_all.27.refs_0_ = bf16[8,88,128]{2,1,0:T(8,128)(2,1)S(1)} all-to-all(bf16[8,88,128]{2,1,0:T(8,128)(2,1)S(1)} %shard_map.150), channel_id=1, replica_groups={{0,2,8,10,32,34,40,42},{4,6,12,14,36,38,44,46},{16,18,24,26,48,50,56,58..., dimensions={0} | all-to-all | bytes 360448 | tf_op jit(solution)/shard_map/all_to_all | solution.py:728
  87.6 0.7 collective-permute-start.9
  88.3 1.3 %collective-permute-start.8 = (bf16[8,88,128]{2,1,0:T(8,128)(2,1)S(1)}, bf16[8,88,128]{2,1,0:T(8,128)(2,1)S(1)}, u32[]{:S(2)}, u32[]{:S(2)}) collective-permute-start(bf16[8,88,128]{2,1,0:T(8,128)(2,1)S(1)} %all_to_all.27.refs_0_), channel_id=1, source_target_pairs={{30,126},{31,127}} | collective-permute-start | bytes 540680 | tf_op jit(solution)/shard_map/ppermute | solution.py:734
  89.6 1.3 %collective-permute-start.7 = (bf16[8,88,128]{2,1,0:T(8,128)(2,1)S(1)}, bf16[8,88,128]{2,1,0:T(8,128)(2,1)S(1)}, u32[]{:S(2)}, u32[]{:S(2)}) collective-permute-start(bf16[8,88,128]{2,1,0:T(8,128)(2,1)S(1)} %all_to_all.27.refs_0_), channel_id=1, source_target_pairs={{102,126},{103,127}} | collective-permute-start | bytes 540680 | tf_op jit(solution)/shard_map/ppermute | solution.py:734
  90.9 1.3 %collective-permute-start.6 = (bf16[8,88,128]{2,1,0:T(8,128)(2,1)S(1)}, bf16[8,88,128]{2,1,0:T(8,128)(2,1)S(1)}, u32[]{:S(2)}, u32[]{:S(2)}) collective-permute-start(bf16[8,88,128]{2,1,0:T(8,128)(2,1)S(1)} %all_to_all.27.refs_0_), channel_id=1, source_target_pairs={{120,126},{121,127}} | collective-permute-start | bytes 540680 | tf_op jit(solution)/shard_map/ppermute | solution.py:734
  92.2 0.0 collective-permute-done.9
  92.2 1.3 %collective-permute-start.13 = (bf16[8,88,128]{2,1,0:T(8,128)(2,1)S(1)}, bf16[8,88,128]{2,1,0:T(8,128)(2,1)S(1)}, u32[]{:S(2)}, u32[]{:S(2)}) collective-permute-start(bf16[8,88,128]{2,1,0:T(8,128)(2,1)S(1)} %collective-permute-done.9), channel_id=1, source_target_pairs={{30,126},{31,127}} | collective-permute-start | bytes 540680 | tf_op jit(solution)/shard_map/ppermute | solution.py:735
  93.5 1.3 %collective-permute-start.12 = (bf16[8,88,128]{2,1,0:T(8,128)(2,1)S(1)}, bf16[8,88,128]{2,1,0:T(8,128)(2,1)S(1)}, u32[]{:S(2)}, u32[]{:S(2)}) collective-permute-start(bf16[8,88,128]{2,1,0:T(8,128)(2,1)S(1)} %collective-permute-done.9), channel_id=1, source_target_pairs={{94,126},{95,127}} | collective-permute-start | bytes 540680 | tf_op jit(solution)/shard_map/ppermute | solution.py:735
  94.8 2.1 %collective-permute-done.8.refs_3_ = bf16[8,88,128]{2,1,0:T(8,128)(2,1)S(1)} collective-permute-done((bf16[8,88,128]{2,1,0:T(8,128)(2,1)S(1)}, bf16[8,88,128]{2,1,0:T(8,128)(2,1)S(1)}, u32[]{:S(2)}, u32[]{:S(2)}) %collective-permute-start.8) | collective-permute-done | bytes 180256 | tf_op jit(solution)/shard_map/ppermute | solution.py:734
  96.9 1.3 %collective-permute-start.11 = (bf16[8,88,128]{2,1,0:T(8,128)(2,1)S(1)}, bf16[8,88,128]{2,1,0:T(8,128)(2,1)S(1)}, u32[]{:S(2)}, u32[]{:S(2)}) collective-permute-start(bf16[8,88,128]{2,1,0:T(8,128)(2,1)S(1)} %collective-permute-done.9), channel_id=1, source_target_pairs={{118,126},{119,127}} | collective-permute-start | bytes 540680 | tf_op jit(solution)/shard_map/ppermute | solution.py:735
  98.2 0.0 collective-permute-done.7.refs_2_
  98.2 1.3 %collective-permute-start.10 = (bf16[8,88,128]{2,1,0:T(8,128)(2,1)S(1)}, bf16[8,88,128]{2,1,0:T(8,128)(2,1)S(1)}, u32[]{:S(2)}, u32[]{:S(2)}) collective-permute-start(bf16[8,88,128]{2,1,0:T(8,128)(2,1)S(1)} %collective-permute-done.9), channel_id=1, source_target_pairs={{124,126},{125,127}} | collective-permute-start | bytes 540680 | tf_op jit(solution)/shard_map/ppermute | solution.py:735
  99.5 0.0 collective-permute-done.6.refs_1_
  99.5 5.8 %collective-permute-done.13.refs_7_ = bf16[8,88,128]{2,1,0:T(8,128)(2,1)S(1)} collective-permute-done((bf16[8,88,128]{2,1,0:T(8,128)(2,1)S(1)}, bf16[8,88,128]{2,1,0:T(8,128)(2,1)S(1)}, u32[]{:S(2)}, u32[]{:S(2)}) %collective-permute-start.13) | collective-permute-done | bytes 180256 | tf_op jit(solution)/shard_map/ppermute | solution.py:735
  105.3 0.0 collective-permute-done.12.refs_6_
  105.3 0.3 collective-permute-done.10.refs_4_
  105.6 1.4 %shard_map.151 = bf16[5184,128]{1,0:T(8,128)(2,1)} custom-call(bf16[8,88,128]{2,1,0:T(8,128)(2,1)S(1)} %all_to_all.27.refs_0_, bf16[8,88,128]{2,1,0:T(8,128)(2,1)S(1)} %collective-permute-done.6.refs_1_, bf16[8,88,128]{2,1,0:T(8,128)(2,1)S(1)} %collective-permute-done.7.refs_2_, ...), custom_call_target="tpu_custom_call", output_to_operand_aliasing={{}: (8, {})} | custom-call | tf_op jit(solution)/shard_map/pallas_call | solution.py:634
  (24 shorter events, 0.1 us)
Async XLA Ops:
  0.0 17.5 %copy-start = (bf16[1296,4,128]{2,1,0:T(4,128)(2,1)S(1)}, bf16[1296,4,128]{2,1,0:T(4,128)(2,1)}, u32[]{:S(2)}) copy-start(bf16[1296,4,128]{2,1,0:T(4,128)(2,1)} %param.15) | copy-start | bytes 3981316
  2.4 15.0 %collective-permute-start.1 = (bf16[1296,128]{1,0:T(8,128)(2,1)}, bf16[1296,128]{1,0:T(8,128)(2,1)S(1)}, u32[]{:S(2)}, u32[]{:S(2)}) collective-permute-start(bf16[1296,128]{1,0:T(8,128)(2,1)} %get-tuple-element.15), channel_id=1, source_target_pairs={{126,124},{127,125}} | collective-permute-start | bytes 995336 | tf_op jit(solution)/shard_map/ppermute | solution.py:695
  5.2 12.3 %collective-permute-start.2 = (bf16[1296,128]{1,0:T(8,128)(2,1)}, bf16[1296,128]{1,0:T(8,128)(2,1)S(1)}, u32[]{:S(2)}, u32[]{:S(2)}) collective-permute-start(bf16[1296,128]{1,0:T(8,128)(2,1)} %get-tuple-element.16), channel_id=1, source_target_pairs={{126,118},{127,119}} | collective-permute-start | bytes 995336 | tf_op jit(solution)/shard_map/ppermute | solution.py:695
  6.5 11.0 %collective-permute-start.3 = (bf16[1296,128]{1,0:T(8,128)(2,1)}, bf16[1296,128]{1,0:T(8,128)(2,1)S(1)}, u32[]{:S(2)}, u32[]{:S(2)}) collective-permute-start(bf16[1296,128]{1,0:T(8,128)(2,1)} %get-tuple-element.17), channel_id=1, source_target_pairs={{126,94},{127,95}} | collective-permute-start | bytes 995336 | tf_op jit(solution)/shard_map/ppermute | solution.py:695
  7.8 14.2 %all-to-all-start = ((s32[64,1,128]{2,1,0:T(1,128)}), s32[64,1,128]{2,1,0:T(1,128)S(1)}, u32[]{:S(2)}, u32[]{:S(2)}) async-start(s32[64,1,128]{2,1,0:T(1,128)} %bitcast.20), calls=%async_computation | async-start | bytes 65536 | tf_op jit(solution)/shard_map/all_to_all | solution.py:696
  17.9 15.6 %copy-start.1 = (f32[4,128]{1,0:T(4,128)S(1)}, f32[4,128]{1,0:T(4,128)}, u32[]{:S(2)}) copy-start(f32[4,128]{1,0:T(4,128)} %depth_ref.3) | copy-start | bytes 6148
  17.9 15.6 %copy-start.2 = (s32[4,128]{1,0:T(4,128)S(1)}, s32[4,128]{1,0:T(4,128)}, u32[]{:S(2)}) copy-start(s32[4,128]{1,0:T(4,128)} %wet_ref.3) | copy-start | bytes 6148
  17.9 15.6 %copy-start.3 = (s32[4,128]{1,0:T(4,128)S(1)}, s32[4,128]{1,0:T(4,128)}, u32[]{:S(2)}) copy-start(s32[4,128]{1,0:T(4,128)} %frac_ref.3) | copy-start | bytes 6148
  22.0 17.7 %copy-start.12 = (s32[1296]{0:T(1024)S(1)}, s32[1296]{0:T(1024)}, u32[]{:S(2)}) copy-start(s32[1296]{0:T(1024)} %param.22) | copy-start | bytes 15556
  22.0 17.7 %copy-start.13 = (s32[1296]{0:T(1024)S(1)}, s32[1296]{0:T(1024)}, u32[]{:S(2)}) copy-start(s32[1296]{0:T(1024)} %param.21) | copy-start | bytes 15556
  23.4 17.5 %copy-start.4 = (s32[4,128]{1,0:T(4,128)S(1)}, s32[4,128]{1,0:T(4,128)}, u32[]{:S(2)}) copy-start(s32[4,128]{1,0:T(4,128)} %target_ref.1) | copy-start | bytes 6148
  23.4 17.5 %copy-start.5 = (f32[36]{0:T(128)S(1)}, f32[36]{0:T(128)}, u32[]{:S(2)}) copy-start(f32[36]{0:T(128)} %coef_ref.1) | copy-start | bytes 436
  23.4 17.5 %copy-start.6 = (f32[144,128]{1,0:T(8,128)S(1)}, f32[144,128]{1,0:T(8,128)}, u32[]{:S(2)}) copy-start(f32[144,128]{1,0:T(8,128)} %constant.19.clone.sin_ref) | copy-start | bytes 221188
  23.4 17.5 %copy-start.7 = (f32[144,128]{1,0:T(8,128)S(1)}, f32[144,128]{1,0:T(8,128)}, u32[]{:S(2)}) copy-start(f32[144,128]{1,0:T(8,128)} %constant.18.clone.cos_ref) | copy-start | bytes 221188
  23.4 17.5 %copy-start.8 = (bf16[2,16,768]{2,1,0:T(8,128)(2,1)S(1)}, bf16[2,16,768]{2,1,0:T(8,128)(2,1)}, u32[]{:S(2)}) copy-start(bf16[2,16,768]{2,1,0:T(8,128)(2,1)} %constant.17.clone.spot_ref) | copy-start | bytes 147460
  23.4 17.5 %copy-start.9 = (f32[72,128]{1,0:T(8,128)S(1)}, f32[72,128]{1,0:T(8,128)}, u32[]{:S(2)}) copy-start(f32[72,128]{1,0:T(8,128)} %constant.21.clone.sinb_ref) | copy-start | bytes 110596
  23.4 17.5 %copy-start.10 = (f32[72,128]{1,0:T(8,128)S(1)}, f32[72,128]{1,0:T(8,128)}, u32[]{:S(2)}) copy-start(f32[72,128]{1,0:T(8,128)} %constant.20.clone.cosb_ref) | copy-start | bytes 110596
  23.5 17.5 %copy-start.11 = (f32[36]{0:T(128)S(1)}, f32[36]{0:T(128)}, u32[]{:S(2)}) copy-start(f32[36]{0:T(128)} %constant.16.clone.speed_ref) | copy-start | bytes 436
  23.5 16.1 %all-to-all-start.1 = ((bf16[64,8,324]{2,1,0:T(8,128)(2,1)}), bf16[64,8,324]{2,1,0:T(8,128)(2,1)S(1)}, u32[]{:S(2)}, u32[]{:S(2)}) async-start(bf16[64,8,324]{2,1,0:T(8,128)(2,1)} %shard_map.148), calls=%async_computation.1 | async-start | bytes 786432 | tf_op jit(solution)/shard_map/all_to_all | solution.py:700
  34.3 5.5 %collective-permute-start = (bf16[2,1296,128]{2,1,0:T(8,128)(2,1)S(1)}, bf16[2,1296,128]{2,1,0:T(8,128)(2,1)S(1)}, u32[]{:S(2)}, u32[]{:S(2)}) collective-permute-start(bf16[2,1296,128]{2,1,0:T(8,128)(2,1)S(1)} %get-tuple-element.13), channel_id=1, source_target_pairs={{0,1},{1,0},{2,3},{3,2},{4,5},{5,4},{6,7},{7,6},{8,9},{9,8},{10,11... | collective-permute-start | bytes 1990664 | tf_op jit(solution)/shard_map/ppermute | solution.py:676
  34.4 5.4 %collective-permute-start.5 = (f32[8,128]{1,0:T(8,128)S(1)}, f32[8,128]{1,0:T(8,128)S(1)}, u32[]{:S(2)}, u32[]{:S(2)}) collective-permute-start(f32[8,128]{1,0:T(8,128)S(1)} %get-tuple-element.18), channel_id=1, source_target_pairs={{0,1},{1,0},{2,3},{3,2},{4,5},{5,4},{6,7},{7,6},{8,9},{9,8},{10,11... | collective-permute-start | bytes 12296 | tf_op jit(solution)/shard_map/ppermute | solution.py:676
  39.6 1.3 %collective-permute-start.4 = (bf16[8,1296]{1,0:T(8,128)(2,1)S(1)}, bf16[8,1296]{1,0:T(8,128)(2,1)S(1)}, u32[]{:S(2)}, u32[]{:S(2)}) collective-permute-start(bf16[8,1296]{1,0:T(8,128)(2,1)S(1)} %concatenate.3.edge_ref), channel_id=1, source_target_pairs={{0,1},{1,0},{2,3},{3,2},{4,5},{5,4},{6,7},{7,6},{8,9},{9,8},{10,11... | collective-permute-start | bytes 62216 | tf_op jit(solution)/shard_map/ppermute | solution.py:676
  87.6 4.6 %collective-permute-start.9 = (bf16[8,88,128]{2,1,0:T(8,128)(2,1)S(1)}, bf16[8,88,128]{2,1,0:T(8,128)(2,1)S(1)}, u32[]{:S(2)}, u32[]{:S(2)}) collective-permute-start(bf16[8,88,128]{2,1,0:T(8,128)(2,1)S(1)} %all_to_all.27.refs_0_), channel_id=1, source_target_pairs={{98,124},{14,118},{56,94},{0,30},{99,125},{15,119},{57,95},{1,31}} | collective-permute-start | bytes 540680 | tf_op jit(solution)/shard_map/ppermute | solution.py:733
  88.3 8.6 %collective-permute-start.8 = (bf16[8,88,128]{2,1,0:T(8,128)(2,1)S(1)}, bf16[8,88,128]{2,1,0:T(8,128)(2,1)S(1)}, u32[]{:S(2)}, u32[]{:S(2)}) collective-permute-start(bf16[8,88,128]{2,1,0:T(8,128)(2,1)S(1)} %all_to_all.27.refs_0_), channel_id=1, source_target_pairs={{30,126},{31,127}} | collective-permute-start | bytes 540680 | tf_op jit(solution)/shard_map/ppermute | solution.py:734
  89.6 8.6 %collective-permute-start.7 = (bf16[8,88,128]{2,1,0:T(8,128)(2,1)S(1)}, bf16[8,88,128]{2,1,0:T(8,128)(2,1)S(1)}, u32[]{:S(2)}, u32[]{:S(2)}) collective-permute-start(bf16[8,88,128]{2,1,0:T(8,128)(2,1)S(1)} %all_to_all.27.refs_0_), channel_id=1, source_target_pairs={{102,126},{103,127}} | collective-permute-start | bytes 540680 | tf_op jit(solution)/shard_map/ppermute | solution.py:734
  90.9 8.6 %collective-permute-start.6 = (bf16[8,88,128]{2,1,0:T(8,128)(2,1)S(1)}, bf16[8,88,128]{2,1,0:T(8,128)(2,1)S(1)}, u32[]{:S(2)}, u32[]{:S(2)}) collective-permute-start(bf16[8,88,128]{2,1,0:T(8,128)(2,1)S(1)} %all_to_all.27.refs_0_), channel_id=1, source_target_pairs={{120,126},{121,127}} | collective-permute-start | bytes 540680 | tf_op jit(solution)/shard_map/ppermute | solution.py:734
  92.2 13.1 %collective-permute-start.13 = (bf16[8,88,128]{2,1,0:T(8,128)(2,1)S(1)}, bf16[8,88,128]{2,1,0:T(8,128)(2,1)S(1)}, u32[]{:S(2)}, u32[]{:S(2)}) collective-permute-start(bf16[8,88,128]{2,1,0:T(8,128)(2,1)S(1)} %collective-permute-done.9), channel_id=1, source_target_pairs={{30,126},{31,127}} | collective-permute-start | bytes 540680 | tf_op jit(solution)/shard_map/ppermute | solution.py:735
  93.5 11.8 %collective-permute-start.12 = (bf16[8,88,128]{2,1,0:T(8,128)(2,1)S(1)}, bf16[8,88,128]{2,1,0:T(8,128)(2,1)S(1)}, u32[]{:S(2)}, u32[]{:S(2)}) collective-permute-start(bf16[8,88,128]{2,1,0:T(8,128)(2,1)S(1)} %collective-permute-done.9), channel_id=1, source_target_pairs={{94,126},{95,127}} | collective-permute-start | bytes 540680 | tf_op jit(solution)/shard_map/ppermute | solution.py:735
  96.9 8.4 %collective-permute-start.11 = (bf16[8,88,128]{2,1,0:T(8,128)(2,1)S(1)}, bf16[8,88,128]{2,1,0:T(8,128)(2,1)S(1)}, u32[]{:S(2)}, u32[]{:S(2)}) collective-permute-start(bf16[8,88,128]{2,1,0:T(8,128)(2,1)S(1)} %collective-permute-done.9), channel_id=1, source_target_pairs={{118,126},{119,127}} | collective-permute-start | bytes 540680 | tf_op jit(solution)/shard_map/ppermute | solution.py:735
  98.2 7.4 %collective-permute-start.10 = (bf16[8,88,128]{2,1,0:T(8,128)(2,1)S(1)}, bf16[8,88,128]{2,1,0:T(8,128)(2,1)S(1)}, u32[]{:S(2)}, u32[]{:S(2)}) collective-permute-start(bf16[8,88,128]{2,1,0:T(8,128)(2,1)S(1)} %collective-permute-done.9), channel_id=1, source_target_pairs={{124,126},{125,127}} | collective-permute-start | bytes 540680 | tf_op jit(solution)/shard_map/ppermute | solution.py:735
